TPU v7x, 512 devices: a whole 4x8x8 slice. The times are simulated.
512 devices in a mesh: pipe: 4 (over z_lo), lon: 32 (over x, y), lat: 4 (over z_hi, core).
Axes of the slice: x: 4, y: 8, z: 8 (z_hi: 2, z_lo: 4; z = z_hi * 4 + z_lo), core: 2. Of those that a mesh axis runs over, the one named last changes fastest.
Arguments:
- acts: bfloat16 [4, 2, 24, 768, 512], P('pipe', None, 'lat', 'lon'), may hold values from -6 to 6
- section_grads: bfloat16 [4, 2, 24, 768, 512], P('pipe', None, 'lat', 'lon'), may hold values from -6 to 6
- gain: float32 [4, 512], P('pipe'), may hold values from 0.1 to 1.9
- w_qkv: bfloat16 [4, 512, 1536], P('pipe'), may hold values from -0.25 to 0.25
- w_out: bfloat16 [4, 512, 512], P('pipe'), may hold values from -0.25 to 0.25
- labels: int32 [24, 768], replicated, may hold values from 0 to 7, as said below
Outputs:
- grad_input: bfloat16 [4, 2, 24, 768, 512], P('pipe', None, 'lat', 'lon')
- grad_wo: float32 [2048, 512], P(('pipe', 'lon', 'lat'))
Inputs may be any that keep to these rules, and one draw needn't show every extreme that they name: `labels`: A cell's label is b + 2 r: b is 1 on the first latitude rows of the initial grid (1 to 3 rows, drawn for each longitude), else 0; r is a region number of 0 to 3 drawn for each cell. A token attends to the tokens of its window that carry the same label.
All inputs are finite; a program needn't handle non-finite values.
Results may differ from a plain program's by a relative error of at most 0.0095.
Values may be sent and summed in bfloat16 or wider, within the bound.
A program may use at most 64 MiB of HBM per device.

v0:
```python
import jax
import jax.numpy as jnp
from jax import lax
from jax.sharding import PartitionSpec as P

HEAD_DIM = 64
WIN_LAT = 6
WIN_LON = 12
SHIFT_LAT = 3
SHIFT_LON = 6


epsilon = 1e-05
masked_score = -1e30


def shifted(array, axis, by):
    count = lax.axis_size(axis)
    return lax.ppermute(array, axis, [(i, (i + by) % count) for i in range(count)])


def for_sending(array):

    def short(part):
        return part.astype(jnp.bfloat16) if part.dtype == jnp.float32 else part

    return jax.tree.map(short, array)


def to_windows(layer_field):
    level_count, row_count, col_count, features = layer_field.shape
    lat_windows = row_count // WIN_LAT
    lon_windows = col_count // WIN_LON
    blocks = layer_field.reshape(level_count, lat_windows, WIN_LAT, lon_windows, WIN_LON, features)
    blocks = blocks.transpose(1, 3, 0, 2, 4, 5)
    return blocks.reshape(lat_windows * lon_windows, level_count * WIN_LAT * WIN_LON, features)


def from_windows(blocks, level_count, row_count, col_count):
    features = blocks.shape[-1]
    lat_windows = row_count // WIN_LAT
    lon_windows = col_count // WIN_LON
    layer_field = blocks.reshape(lat_windows, lon_windows, level_count, WIN_LAT, WIN_LON, features)
    return layer_field.transpose(2, 0, 3, 1, 4, 5).reshape(
        level_count, row_count, col_count, features
    )


def multiply(form, left, right):
    return jnp.einsum(form, left, right, preferred_element_type=jnp.float32)


def normalize(layer_input, gain_row):
    values_f = layer_input.astype(jnp.float32)
    mean_value = jnp.mean(values_f, -1, keepdims=True)
    variance = jnp.mean((values_f - mean_value) ** 2, -1, keepdims=True)
    inverse = 1.0 / jnp.sqrt(variance + epsilon)
    centred = (values_f - mean_value) * inverse
    return ((centred * gain_row).astype(jnp.bfloat16), centred, inverse)


def project_rows(normed, weight_in):
    lead = normed.shape[:-1]
    width = weight_in.shape[0]
    projected = jnp.dot(normed.reshape(-1, width), weight_in, preferred_element_type=jnp.float32)
    return projected.astype(jnp.bfloat16).reshape(lead + (3 * width,))


def attend_backward(projected, upstream, label_win, weight_out):
    window_count, token_count, triple = projected.shape
    width = triple // 3
    head_count = width // HEAD_DIM
    split_heads = projected.reshape(window_count, token_count, 3, head_count, HEAD_DIM)
    queries = split_heads[:, :, 0]
    key_rows = split_heads[:, :, 1]
    value_rows = split_heads[:, :, 2]
    score_scale = HEAD_DIM ** (-0.5)
    scores = multiply("wqhe,wkhe->whqk", queries, key_rows) * score_scale
    same_label = (label_win[:, :, None] == label_win[:, None, :])[:, None]
    scores = jnp.where(same_label, scores, masked_score)
    row_peak = jnp.max(scores, -1, keepdims=True)
    exps = jnp.exp(scores - row_peak)
    weights = exps / jnp.sum(exps, -1, keepdims=True)
    weights_low = weights.astype(jnp.bfloat16)
    attended = multiply("whqk,wkhe->wqhe", weights_low, value_rows).astype(jnp.bfloat16)
    attended = attended.reshape(window_count, token_count, width)
    grad_attended = multiply("wtd,ed->wte", upstream, weight_out).astype(jnp.bfloat16)
    grad_heads = grad_attended.reshape(window_count, token_count, head_count, HEAD_DIM)
    grad_weights = multiply("wqhe,wkhe->whqk", grad_heads, value_rows)
    inner = jnp.sum(grad_weights * weights, -1, keepdims=True)
    grad_scores = (weights * (grad_weights - inner) * score_scale).astype(jnp.bfloat16)
    grad_query = multiply("whqk,wkhe->wqhe", grad_scores, key_rows)
    grad_keys = multiply("whqk,wqhe->wkhe", grad_scores, queries)
    grad_values = multiply("whqk,wqhe->wkhe", weights_low, grad_heads)
    grad_proj = jnp.stack([grad_query, grad_keys, grad_values], 2).astype(jnp.bfloat16)
    return (grad_proj.reshape(window_count, token_count, triple), attended)


def norm_backward(grad_proj, weight_in, gain_row, centred, inverse):
    width = weight_in.shape[0]
    lead = grad_proj.shape[:-1]
    grad_normed = jnp.dot(
        grad_proj.reshape(-1, 3 * width), weight_in.T, preferred_element_type=jnp.float32
    )
    scaled = grad_normed.reshape(lead + (width,)) * gain_row
    first = jnp.mean(scaled, -1, keepdims=True)
    second = jnp.mean(scaled * centred, -1, keepdims=True)
    return inverse * (scaled - first - centred * second)


def extend_inputs(arrays):
    margins = tuple((item[:, :, :SHIFT_LON] for item in arrays))
    from_right = shifted((margins[0], margins[1]), "lon", -1)
    widened = [
        jnp.concatenate([item[:, :, SHIFT_LON:], extra], 2)
        for item, extra in zip(arrays, from_right)
    ]
    upper_rows = shifted((widened[0][:, :SHIFT_LAT], widened[1][:, :SHIFT_LAT]), "lat", -1)
    return tuple(
        (
            jnp.concatenate([item[:, SHIFT_LAT:], extra], 1)
            for item, extra in zip(widened, upper_rows)
        )
    )


def fold_inputs(region):
    row_count = region.shape[1]
    col_count = region.shape[2]
    from_below = shifted(region[:, row_count - SHIFT_LAT :].astype(jnp.bfloat16), "lat", 1).astype(
        jnp.float32
    )
    tall = jnp.concatenate([from_below, region[:, : row_count - SHIFT_LAT]], 1)
    from_left = shifted(for_sending(tall[:, :, col_count - SHIFT_LON :]), "lon", 1)
    return jnp.concatenate([from_left, tall[:, :, : col_count - SHIFT_LON]], 2)


def on_device(acts, section_grads, gain, w_qkv, w_out, labels):
    layer_input = acts[0]
    gain_row = gain[0]
    weight_in = w_qkv[0]
    weight_out = w_out[0]
    level_count, row_count, col_count, width = layer_input.shape
    upstream = shifted(section_grads[0], "pipe", -1)
    lat_index = lax.axis_index("lat")
    lon_index = lax.axis_index("lon")
    rolled_labels = jnp.roll(labels, (-SHIFT_LAT, -SHIFT_LON), (0, 1))
    labels_here = lax.dynamic_slice(
        rolled_labels, (lat_index * row_count, lon_index * col_count), (row_count, col_count)
    )
    label_field = jnp.broadcast_to(
        labels_here[None, :, :, None], (level_count, row_count, col_count, 1)
    )
    label_win = to_windows(label_field)[..., 0]
    region_input, region_grad = extend_inputs((layer_input, upstream))
    normed, centred, inverse = normalize(region_input, gain_row)
    projected = project_rows(normed, weight_in)
    grad_win, attended = attend_backward(
        to_windows(projected), to_windows(region_grad), label_win, weight_out
    )
    attended_flat = attended.reshape(-1, width)
    grad_flat = to_windows(region_grad).reshape(-1, width)
    wo_share = lax.psum_scatter(
        jnp.einsum("te,td->ed", attended_flat, grad_flat, preferred_element_type=jnp.float32),
        ("lon", "lat"),
        scatter_dimension=0,
        tiled=True,
    )
    grad_proj = from_windows(grad_win, level_count, row_count, col_count)
    branch = norm_backward(grad_proj, weight_in, gain_row, centred, inverse)
    branch = fold_inputs(branch)
    summed = (upstream.astype(jnp.float32) + branch).astype(jnp.bfloat16)
    return (summed[None], wo_share)


def solution(mesh):
    in_specs = (
        P("pipe", None, "lat", "lon", None),
        P("pipe", None, "lat", "lon", None),
        P("pipe", None),
        P("pipe", None, None),
        P("pipe", None, None),
        P(),
    )
    out_specs = (P("pipe", None, "lat", "lon", None), P(("pipe", "lon", "lat"), None))
    return jax.shard_map(
        on_device, mesh=mesh, in_specs=in_specs, out_specs=out_specs, check_vma=False
    )
```

profile of v0, /device:TPU:1, one launch (start us, length us, event | category | flops | bytes accessed | tf_op | source)
XLA Modules:
  0.0 1649.3 jit_solution(11952779481191845672)
XLA Ops:
  7.2 1.0 slice.83
  8.2 8.1 collective-permute-start.1
  16.4 7.6 collective-permute-start
  24.0 0.9 slice.68
  24.9 0.7 slice.69
  25.9 1.0 slice.82
  27.1 3.1 collective-permute-start.2
  30.3 0.7 broadcast_compare_fusion
  31.0 9.7 collective-permute-done.2
  41.5 1.5 convolution_convert_fusion
  43.1 1.3 reshape_reshape.14
  44.4 1.8 copy.34
  46.2 3.1 reshape_reshape.15
  49.3 1.3 fusion.88
  50.7 1.5 copy.59
  52.2 1.7 copy.60
  53.9 1.0 slice.91
  55.0 2.1 collective-permute-start.3
  57.0 3.3 fusion.89
  60.4 0.5 copy.61
  60.9 1.0 slice.90
  61.9 1.6 fusion.74
  63.5 2.1 collective-permute-start.4
  65.6 2.0 fusion.25
  67.7 0.4 copy.51
  68.0 0.3 reshape_reshape.16
  68.4 7.4 collective-permute-done.4
  75.8 1.0 pad_maximum_fusion.3
  77.4 1.1 convolution_convert_fusion.3
  78.5 1.2 copy.58
  79.7 1.9 fusion.54
  81.6 5.7 fusion.29
  87.3 5.5 fusion.26
  92.7 3.0 fusion.24
  95.8 1.5 fusion.94
  97.3 2.6 pad_maximum_fusion
  99.9 3.3 copy.47
  103.1 1.9 convert_element_type.75
  105.1 2.1 copy.48
  107.2 1.7 fusion.87
  109.2 1.9 collective-permute-start.5
  111.1 3.6 collective-permute-done.5
  114.8 2.2 collective-permute-start.6
  117.0 1.3 dynamic-slice
  118.9 4.6 collective-permute-done.6
  123.5 1.8 fusion.62
  125.3 1515.9 %all-reduce.3.cloned.1.call-done = f32[512,512]{1,0:T(8,128)} async-done(((f32[512,512]{1,0:T(8,128)}), f32[512,512]{1,0:T(8,128)}) %all-reduce.3.cloned.1.call-update) | async-done | bytes 1048592
  1641.2 1.3 constant_dynamic-slice_fusion
  (55 shorter events, 2.3 us)
Async XLA Ops:
  7.2 34.3 %copy-start = (bf16[1,512,1536]{2,1,0:T(8,128)(2,1)S(1)}, bf16[1,512,1536]{2,1,0:T(8,128)(2,1)}, u32[]{:S(2)}) copy-start(bf16[1,512,1536]{2,1,0:T(8,128)(2,1)} %param.9) | copy-start | bytes 4718596
  7.2 34.2 %copy-start.10 = (f32[1,512]{1,0:T(1,128)S(1)}, f32[1,512]{1,0:T(1,128)}, u32[]{:S(2)}) copy-start(f32[1,512]{1,0:T(1,128)} %param.8) | copy-start | bytes 6148
  7.2 1634.0 %all-reduce.3.cloned.1.call-start = ((), (), s32[]{:S(2)}) async-start(), calls=%async_computation | async-start | bytes 2097152
  8.2 18.8 %collective-permute-start.1 = (bf16[2,6,6,512]{3,2,1,0:T(8,128)(2,1)S(1)}, bf16[2,6,6,512]{3,2,1,0:T(8,128)(2,1)S(1)}, u32[]{:S(2)}, u32[]{:S(2)}) collective-permute-start(bf16[2,6,6,512]{3,2,1,0:T(8,128)(2,1)S(1)} %slice.83), channel_id=1, source_target_pairs={{0,124},{4,0},{8,4},{12,8},{16,12},{20,16},{24,20},{28,24},{32,28}... | collective-permute-start | bytes 221192 | tf_op jit(solution)/shard_map/ppermute | solution.py:19
  16.4 37.6 %collective-permute-start = (bf16[2,6,24,512]{3,2,1,0:T(8,128)(2,1)}, bf16[2,6,24,512]{3,2,1,0:T(8,128)(2,1)}, u32[]{:S(2)}, u32[]{:S(2)}) collective-permute-start(bf16[2,6,24,512]{3,2,1,0:T(8,128)(2,1)} %bitcast.107), channel_id=1, source_target_pairs={{0,384},{128,0},{256,128},{384,256},{1,385},{129,1},{257,129},{385... | collective-permute-start | bytes 884744 | tf_op jit(solution)/shard_map/ppermute | solution.py:19
  27.1 13.6 collective-permute-start.2
  40.7 0.7 copy-start.2
  52.2 8.2 copy-start.5
  53.9 6.5 copy-start.6
  55.0 5.4 copy-start.1
  55.0 7.0 collective-permute-start.3
  60.4 7.3 copy-start.11
  63.5 12.3 collective-permute-start.4
  68.4 9.1 copy-start.4
  81.6 5.7 copy-start.7
  81.6 5.7 copy-start.12
  95.7 1.6 copy-start.8
  95.8 1.5 copy-start.9
  107.2 1.8 copy-start.3
  109.2 5.5 collective-permute-start.5
  114.8 8.7 collective-permute-start.6
Sparse Core Ops, SparseCore 0:
  97.4 1543.7 all-reduce.2
where the time goes:
time: 1650 us
  waiting for transfers between devices  1540 us (93%)
  local copies, waits for them, and re-layouts  30 us (2%)
  starting transfers between devices  27.1 us (2%)
  matrix products  27.1 us (2%)
    unnamed x2, waiting for transfers between devices  1520 us
  transfers between devices with their start and end apart: 8, of which 5 were waited for; matrix products, arithmetic and copies ran while one was open for 2% of the time, Pallas kernels for 0%

commit v1 on v0

v1 whole, which is shorter than its diff:
```python
import functools

import jax
import jax.numpy as jnp
import numpy as np
from jax import lax
from jax.experimental import pallas as pl
from jax.experimental.pallas import tpu as pltpu
from jax.sharding import PartitionSpec as P

MESH = pl.DeviceIdType.MESH
LEV = 2
LAT_CELLS = 6
LON_CELLS = 24
TOKENS = 288
WIN = 144
D = 512
GROUP = 256
HEADS = 4
COLS = HEADS * WIN
SEND = 320
R00 = (0, 112)
R10 = (112, 112)
R01 = (224, 48)
R11 = (272, 48)
epsilon = 1e-05
masked_score = -1e30
open_score = 3e38


def natural(lev, row, col):
    return (lev * LAT_CELLS + row) * LON_CELLS + col


def group_cells(upper, left, part):
    rows = range(0, 3) if upper else range(3, 6)
    if left:
        cols = range(0, 6)
    else:
        cols = range(6, 18) if part == 0 else range(18, 24)
    return [(l, r, c) for l in range(LEV) for r in rows for c in cols]


def layouts():
    sent = {}
    for name, upper, left, start in (("00", 0, 0, 0), ("10", 1, 0, 112), ("01", 0, 1, 224), ("11", 1, 1, 272)):
        at = start
        for part in range(1 if left else 2):
            for cell in group_cells(upper, left, part):
                sent[(name, part if not left else 1, cell)] = at
                at += 1
    p_send = np.zeros((SEND, TOKENS), np.float32)
    for (name, part, cell), at in sent.items():
        p_send[at, natural(*cell)] = 1
    order = []
    for name, upper, left, part in (
        ("00", 0, 0, 0),
        ("10", 1, 0, 0),
        ("00", 0, 0, 1),
        ("10", 1, 0, 1),
        ("01", 0, 1, 1),
        ("11", 1, 1, 1),
    ):
        for cell in group_cells(upper, left, part):
            order.append((name, part, cell))
    p_win = np.zeros((TOKENS, SEND), np.float32)
    rows = np.zeros((TOKENS, 24), np.float32)
    cols = np.zeros((TOKENS, 128), np.float32)
    for t, (name, part, cell) in enumerate(order):
        p_win[t, sent[(name, part, cell)]] = 1
        rows[t, cell[1] + (6 if name[0] == "1" else 0)] = 1
        cols[t, cell[2] + (24 if name[1] == "1" else 0)] = 1
    return p_send, p_win, rows, cols


def dot(left, right, dims=((1,), (0,))):
    return lax.dot_general(left, right, (dims, ((), ())), preferred_element_type=jnp.float32)


NT = ((1,), (1,))
TN = ((0,), (0,))


def kernel(
    sizes,
    acts_hbm, grads_hbm, gain_hbm, wqkv_hbm, wout_hbm, labels_hbm,
    psend_hbm, pwin_hbm, pret_hbm, pout_hbm, rows_hbm, cols_hbm,
    out_ref, wo_ref,
    acts_v, grads_v, gain_v, wqkv_v, wout_v, labels_v,
    psend_v, pwin_v, pret_v, pout_v, rows_v, cols_v,
    acts_send, acts_recv, grads_send, grads_recv, ret_send, ret_recv,
    mask_v, perm_v, qkv_v, qb_v, w_v, wl_v, att_v, up_v, ga_v, gb_v, gp_v, cen_v, inv_v,
    own_v, a_send, a_recv, b_send, b_recv, c_send, c_recv, d_send, d_recv,
    in_sem, send_sem, recv_sem,
):
    pipe_n, nx, ny, nz = sizes
    lon_n, lat_n = nx * ny, nz * 2
    s = lax.axis_index("pipe")
    j = lax.axis_index("lon")
    i = lax.axis_index("lat")
    x, y = j // ny, j % ny
    z, core = i // 2, i % 2

    def near(ds, dj, di):
        return (
            (s + ds + pipe_n) % pipe_n if ds else s,
            (j + dj + lon_n) % lon_n if dj else j,
            (i + di + lat_n) % lat_n if di else i,
        )

    def on_x(k):
        return (s, ((x + k) % nx) * ny + y, i)

    def on_y(k):
        return (s, x * ny + (y + k) % ny, i)

    twin = (s, j, z * 2 + (1 - core))
    far = (s, j, ((z + 1) % nz) * 2 + core)

    barrier = pltpu.get_barrier_semaphore()
    senders = [near(0, 0, 1), near(0, 1, 0), near(0, 1, 1), near(0, 0, -1), near(0, -1, 0), near(0, -1, -1)]
    senders += [near(1, 0, 0), near(1, 0, 1), near(1, 1, 0), near(1, 1, 1)]
    senders += [twin, far]
    senders += [on_x(k) for k in range(1, nx)] + [on_y(k) for k in range(1, ny)]
    for device in senders:
        pl.semaphore_signal(barrier, inc=1, device_id=device, device_id_type=MESH)

    loads = []
    for n, (src, dst) in enumerate((
        (acts_hbm, acts_v), (psend_hbm, psend_v), (grads_hbm, grads_v), (labels_hbm, labels_v),
        (rows_hbm, rows_v), (cols_hbm, cols_v), (pwin_hbm, pwin_v), (gain_hbm, gain_v),
        (wqkv_hbm, wqkv_v), (wout_hbm, wout_v), (pret_hbm, pret_v), (pout_hbm, pout_v),
    )):
        load = pltpu.make_async_copy(src, dst, in_sem.at[n])
        load.start()
        loads.append(load)
    (l_acts, l_psend, l_grads, l_labels, l_rows, l_cols, l_pwin, l_gain, l_wqkv, l_wout, l_pret, l_pout) = loads

    started = []

    def send(src, dst, device):
        n = len(started)
        copy = pltpu.make_async_remote_copy(
            src_ref=src, dst_ref=dst, send_sem=send_sem.at[n], recv_sem=recv_sem.at[n],
            device_id=device, device_id_type=MESH,
        )
        copy.start()
        started.append(copy)
        return copy

    def rows_of(ref, part):
        return ref.at[pl.ds(part[0], part[1])]

    l_acts.wait()
    l_psend.wait()
    ordered = dot(psend_v[...], acts_v[...]).astype(jnp.bfloat16)
    acts_send[...] = ordered
    acts_recv[0:112, :] = ordered[0:112]
    l_grads.wait()
    grads_send[...] = dot(psend_v[...], grads_v[...]).astype(jnp.bfloat16)

    pl.semaphore_wait(barrier, len(senders))
    acts_in = [
        send(rows_of(acts_send, R10), rows_of(acts_recv, R10), near(0, 0, -1)),
        send(rows_of(acts_send, R11), rows_of(acts_recv, R11), near(0, -1, -1)),
        send(rows_of(acts_send, R01), rows_of(acts_recv, R01), near(0, -1, 0)),
    ]
    grads_in = [
        send(rows_of(grads_send, R10), rows_of(grads_recv, R10), near(-1, 0, -1)),
        send(rows_of(grads_send, R11), rows_of(grads_recv, R11), near(-1, -1, -1)),
        send(rows_of(grads_send, R00), rows_of(grads_recv, R00), near(-1, 0, 0)),
        send(rows_of(grads_send, R01), rows_of(grads_recv, R01), near(-1, -1, 0)),
    ]

    l_labels.wait()
    l_rows.wait()
    l_cols.wait()
    row_n, col_n = labels_v.shape
    cell = lax.broadcasted_iota(jnp.int32, (col_n, 128), 0) - j * LON_CELLS
    cell = jnp.where(cell < 0, cell + col_n, cell)
    pick_col = (cell == lax.broadcasted_iota(jnp.int32, (col_n, 128), 1)).astype(jnp.float32)
    row = lax.broadcasted_iota(jnp.int32, (row_n, row_n), 1) - i * LAT_CELLS
    row = jnp.where(row < 0, row + row_n, row)
    pick_row = (row == lax.broadcasted_iota(jnp.int32, (row_n, row_n), 0)).astype(jnp.float32)
    near_labels = dot(pick_row, dot(labels_v[...].astype(jnp.float32), pick_col))
    token_label = jnp.sum(dot(rows_v[...], near_labels) * cols_v[...], -1, keepdims=True)
    lane = lax.broadcasted_iota(jnp.int32, (TOKENS, 128), 1).astype(jnp.float32)
    one_hot = (token_label == lane).astype(jnp.float32).astype(jnp.bfloat16)
    for w in range(2):
        here = one_hot[w * WIN:(w + 1) * WIN]
        alike = dot(here, jnp.concatenate([here] * HEADS, 0), NT)
        mask_v[w] = jnp.where(alike > 0.5, open_score, masked_score)

    per = D // (2 * nx * ny * nz)
    m = lax.broadcasted_iota(jnp.int32, (D, D), 0)
    r_at = m % per
    z_at = (m // per) % nz
    y_at = (m // (per * nz)) % ny
    x_at = (m // (per * nz * ny)) % nx
    c_at = m // (per * nz * ny * nx)
    feature = (
        (((x_at + x) % nx * ny + (y_at + y) % ny) * nz + (z_at + z) % nz) * 2 + (c_at + core) % 2
    ) * per + r_at
    perm_v[...] = (feature == lax.broadcasted_iota(jnp.int32, (D, D), 1)).astype(jnp.float32).astype(jnp.bfloat16)

    l_pwin.wait()
    l_gain.wait()
    l_wqkv.wait()
    for copy in acts_in:
        copy.wait_recv()
    gain = gain_v[...]
    inputs = dot(pwin_v[...], acts_recv[...])
    mean = jnp.mean(inputs, -1, keepdims=True)
    centred = inputs - mean
    inverse = 1.0 / jnp.sqrt(jnp.mean(centred * centred, -1, keepdims=True) + epsilon)
    centred = centred * inverse
    cen_v[...] = centred
    inv_v[...] = jnp.broadcast_to(inverse, inv_v.shape)
    projected = dot((centred * gain).astype(jnp.bfloat16), wqkv_v[...])
    for part in range(3):
        for w in range(2):
            for g in range(2):
                at = part * D + g * GROUP
                qkv_v[part, w * 2 + g] = projected[w * WIN:(w + 1) * WIN, at:at + GROUP].astype(jnp.bfloat16)

    head_lane = lax.broadcasted_iota(jnp.int32, (1, GROUP), 1) // 64
    head_mask = [(head_lane == h).astype(jnp.float32) for h in range(HEADS)]

    def spread(block, dst, n, scale):
        for h in range(HEADS):
            dst[n, h * WIN:(h + 1) * WIN, :] = (block * (head_mask[h] * scale)).astype(jnp.bfloat16)

    def gather(product):
        total = product[0:WIN] * head_mask[0]
        for h in range(1, HEADS):
            total = total + product[h * WIN:(h + 1) * WIN] * head_mask[h]
        return total

    def forward(n, carry):
        spread(qkv_v[0, n].astype(jnp.float32), qb_v, n, 0.125)
        scores = jnp.minimum(dot(qkv_v[1, n], qb_v[n], NT), mask_v[n // 2])
        exps = jnp.exp(scores - jnp.max(scores, 0, keepdims=True))
        weights = exps * (1.0 / jnp.sum(exps, 0, keepdims=True))
        w_v[n] = weights
        low = weights.astype(jnp.bfloat16)
        wl_v[n] = low
        att_v[n] = gather(dot(low, qkv_v[2, n], TN)).astype(jnp.bfloat16)
        return carry

    lax.fori_loop(0, 4, forward, 0)

    l_wout.wait()
    for copy in grads_in:
        copy.wait_recv()
    upstream = dot(pwin_v[...], grads_recv[...]).astype(jnp.bfloat16)
    up_v[...] = upstream
    attended = jnp.concatenate(
        [jnp.concatenate([att_v[2 * w], att_v[2 * w + 1]], 1) for w in range(2)], 0
    )
    turned = dot(perm_v[...], attended, NT).astype(jnp.bfloat16)
    half = D // 2
    a_send[...] = dot(turned[half:], upstream).astype(jnp.bfloat16)
    step_a = send(a_send, a_recv, twin)
    own_v[...] = dot(turned[:half], upstream)

    grad_att = dot(upstream, wout_v[...], NT)
    for w in range(2):
        for g in range(2):
            ga_v[w * 2 + g] = grad_att[w * WIN:(w + 1) * WIN, g * GROUP:(g + 1) * GROUP].astype(jnp.bfloat16)

    def backward(n, carry):
        spread(ga_v[n].astype(jnp.float32), gb_v, n, 1.0)
        grad_w = dot(qkv_v[2, n], gb_v[n], NT)
        weights = w_v[n]
        inner = jnp.sum(grad_w * weights, 0, keepdims=True)
        grad_s = (weights * (grad_w - inner)).astype(jnp.bfloat16)
        gp_v[0, n] = (gather(dot(grad_s, qkv_v[1, n], TN)) * 0.125).astype(jnp.bfloat16)
        gp_v[1, n] = dot(grad_s, qb_v[n]).astype(jnp.bfloat16)
        gp_v[2, n] = dot(wl_v[n], gb_v[n]).astype(jnp.bfloat16)
        return carry

    lax.fori_loop(0, 2, backward, 0)

    step_a.wait_recv()
    chunk = half // nx
    summed = own_v[...] + a_recv[...].astype(jnp.float32)
    own_v[...] = summed
    b_send[...] = summed.astype(jnp.bfloat16)
    step_b = [
        send(b_send.at[pl.ds(k * chunk, chunk)], b_recv.at[pl.ds((k - 1) * chunk, chunk)], on_x(k))
        for k in range(1, nx)
    ]

    lax.fori_loop(2, 4, backward, 0)

    for copy in step_b:
        copy.wait_recv()
    total = own_v[0:chunk, :]
    for k in range(1, nx):
        total = total + b_recv[(k - 1) * chunk:k * chunk, :].astype(jnp.float32)
    own_v[0:chunk, :] = total
    piece = chunk // ny
    for k in range(1, ny):
        part = total[k * piece:(k + 1) * piece]
        c_send[k] = jnp.concatenate([part[:, :half], part[:, half:]], 0).astype(jnp.bfloat16)
    step_c = [send(c_send.at[k], c_recv.at[k], on_y(k)) for k in range(1, ny)]

    grad_proj = jnp.concatenate(
        [
            jnp.concatenate([gp_v[part, 2 * w + g] for part in range(3) for g in range(2)], 1)
            for w in range(2)
        ],
        0,
    )
    scaled = dot(grad_proj, wqkv_v[...], NT) * gain
    centred = cen_v[...]
    first = jnp.mean(scaled, -1, keepdims=True)
    second = jnp.mean(scaled * centred, -1, keepdims=True)
    branch = inv_v[:, 0:1] * (scaled - first - centred * second)
    result = (up_v[...].astype(jnp.float32) + branch).astype(jnp.bfloat16)
    l_pret.wait()
    back = dot(pret_v[...], result).astype(jnp.bfloat16)
    ret_send[...] = back
    ret_recv[0:112, :] = back[0:112]
    ret_in = [
        send(rows_of(ret_send, R10), rows_of(ret_recv, R10), near(0, 0, 1)),
        send(rows_of(ret_send, R11), rows_of(ret_recv, R11), near(0, 1, 1)),
        send(rows_of(ret_send, R01), rows_of(ret_recv, R01), near(0, 1, 0)),
    ]

    for copy in step_c:
        copy.wait_recv()
    total = own_v[0:piece, :]
    for k in range(1, ny):
        got = c_recv[k].astype(jnp.float32)
        total = total + jnp.concatenate([got[:piece], got[piece:]], 1)
    d_send[...] = total[per:]
    step_d = send(d_send, d_recv, far)

    l_pout.wait()
    for copy in ret_in:
        copy.wait_recv()
    out_ref[...] = dot(pout_v[...], ret_recv[...]).astype(jnp.bfloat16)
    step_d.wait_recv()
    wo_ref[...] = total[:per] + d_recv[...]
    for copy in started:
        copy.wait_send()


def on_device(sizes, acts, section_grads, gain, w_qkv, w_out, labels):
    pipe_n, nx, ny, nz = sizes
    p_send, p_win, rows, cols = layouts()
    low = lambda m: jnp.asarray(m, jnp.bfloat16)
    per = D // (2 * nx * ny * nz)
    half = D // 2
    chunk = half // nx
    piece = chunk // ny
    sends = 3 + 4 + 3 + 1 + (nx - 1) + (ny - 1) + 1
    bf, f32 = jnp.bfloat16, jnp.float32
    vm = pltpu.VMEM
    scratch = [
        vm((TOKENS, D), bf), vm((TOKENS, D), bf), vm((1, D), f32), vm((D, 3 * D), bf), vm((D, D), bf),
        vm(labels.shape, jnp.int32),
        vm((SEND, TOKENS), bf), vm((TOKENS, SEND), bf), vm((SEND, TOKENS), bf), vm((TOKENS, SEND), bf),
        vm((TOKENS, 24), f32), vm((TOKENS, 128), f32),
    ]
    scratch += [vm((SEND, D), bf)] * 6
    scratch += [
        vm((2, WIN, COLS), f32), vm((D, D), bf), vm((3, 4, WIN, GROUP), bf), vm((4, COLS, GROUP), bf),
        vm((4, WIN, COLS), f32), vm((4, WIN, COLS), bf), vm((4, WIN, GROUP), bf), vm((TOKENS, D), bf),
        vm((4, WIN, GROUP), bf), vm((4, COLS, GROUP), bf), vm((3, 4, WIN, GROUP), bf),
        vm((TOKENS, D), f32), vm((TOKENS, 128), f32),
    ]
    scratch += [
        vm((half, D), f32), vm((half, D), bf), vm((half, D), bf), vm((half, D), bf),
        vm(((nx - 1) * chunk, D), bf), vm((ny, 2 * piece, half), bf), vm((ny, 2 * piece, half), bf),
        vm((per, D), f32), vm((per, D), f32),
        pltpu.SemaphoreType.DMA((12,)), pltpu.SemaphoreType.DMA((sends,)), pltpu.SemaphoreType.DMA((sends,)),
    ]
    anywhere = pl.BlockSpec(memory_space=pl.ANY)
    out, wo = pl.pallas_call(
        functools.partial(kernel, sizes),
        out_shape=(jax.ShapeDtypeStruct((TOKENS, D), bf), jax.ShapeDtypeStruct((per, D), f32)),
        in_specs=[anywhere] * 12,
        out_specs=(pl.BlockSpec(memory_space=pltpu.VMEM), pl.BlockSpec(memory_space=pltpu.VMEM)),
        scratch_shapes=scratch,
        compiler_params=pltpu.CompilerParams(
            collective_id=0, has_side_effects=True, vmem_limit_bytes=48 * 1024 * 1024
        ),
        name="sublayer",
    )(
        acts.reshape(TOKENS, D), section_grads.reshape(TOKENS, D), gain, w_qkv[0], w_out[0], labels,
        low(p_send), low(p_win), low(p_win.T), low(p_send.T), jnp.asarray(rows), jnp.asarray(cols),
    )
    return out.reshape(acts.shape), wo


def solution(mesh):
    pipe_n, lon_n, lat_n = (mesh.shape[axis] for axis in ("pipe", "lon", "lat"))
    ny = 8 if lon_n == 32 else min(lon_n, 2)
    sizes = (pipe_n, lon_n // ny, ny, lat_n // 2)
    in_specs = (
        P("pipe", None, "lat", "lon", None),
        P("pipe", None, "lat", "lon", None),
        P("pipe", None),
        P("pipe", None, None),
        P("pipe", None, None),
        P(),
    )
    out_specs = (P("pipe", None, "lat", "lon", None), P(("pipe", "lon", "lat"), None))
    return jax.shard_map(
        functools.partial(on_device, sizes), mesh=mesh, in_specs=in_specs, out_specs=out_specs, check_vma=False
    )
```

time: 1650 us -> 64.4 us (0.04)
  waiting for transfers between devices: 1540 us -> 0 us
  Pallas kernels: 0 us -> 50.5 us
  matrix products: 27.1 us -> 0 us
  starting transfers between devices: 27.1 us -> 0 us
  local copies, waits for them, and re-layouts: 30 us -> 12.8 us
    unnamed x2 -> x0, waiting for transfers between devices: 1520 us -> none
    pallas_call x0 -> x1, Pallas kernels: none -> 50.5 us  [on_device(): pl.pallas_call(functools.partial(kernel, sizes), out_shape=(jax.ShapeDtyp...]
    ppermute x7 -> x0, starting transfers between devices: 27.1 us -> none  [shifted(): lax.ppermute(array, axis, [(i, (i + by) % count) for i in range(count)])]
    ppermute x7 -> x0, waiting for transfers between devices: 25.3 us -> none  [shifted(): lax.ppermute(array, axis, [(i, (i + by) % count) for i in range(count)])]
    dot_general x9 -> x0, matrix products: 23.8 us -> none  [the longest x6 19.1 us: multiply(): return jnp.einsum(form, left, right, preferred_element_type=jnp.float32)]
  transfers between devices with their start and end apart: 8 -> 0, of which waited for: 5 -> 0; matrix products, arithmetic and copies ran while one was open for 2% -> 0% of each run, Pallas kernels for 0% -> 0%
where the time goes in v1:
time: 64.4 us; the launch traced here: 63.9 us
  Pallas kernels  50.5 us (78%)
  local copies, waits for them, and re-layouts  12.8 us (20%)
  between operations  0.66 us (1%)
    pallas_call x1, Pallas kernels, on_device(): pl.pallas_call(functools.partial(kernel, sizes), out_shape=(jax.ShapeDtyp...  50.5 us
    unnamed x26, local copies, waits for them, and re-layouts  12.8 us

profile of v1, /device:TPU:1, one launch (start us, length us, event | category | flops | bytes accessed | tf_op | source)
XLA Modules:
  0.0 63.9 jit_solution(8951684756980854730)
XLA Ops:
  0.6 0.0 copy-start
  0.6 1.4 %copy-done = bf16[1,512,1536]{2,1,0:T(8,128)(2,1)S(1)} copy-done((bf16[1,512,1536]{2,1,0:T(8,128)(2,1)S(1)}, bf16[1,512,1536]{2,1,0:T(8,128)(2,1)}, u32[]{:S(2)}) %copy-start) | copy-done | bytes 1572888
  2.0 0.0 copy-start.1
  2.0 1.0 %copy-done.1 = bf16[1,512,512]{2,1,0:T(8,128)(2,1)S(1)} copy-done((bf16[1,512,512]{2,1,0:T(8,128)(2,1)S(1)}, bf16[1,512,512]{2,1,0:T(8,128)(2,1)}, u32[]{:S(2)}) %copy-start.1) | copy-done | bytes 524312
  3.1 0.0 copy-start.2
  3.1 1.0 %copy-done.2 = bf16[1,2,6,24,512]{4,3,2,1,0:T(8,128)(2,1)S(1)} copy-done((bf16[1,2,6,24,512]{4,3,2,1,0:T(8,128)(2,1)S(1)}, bf16[1,2,6,24,512]{4,3,2,1,0:T(8,128)(2,1)}, u32[]{:S(2)}) %copy-start.2) | copy-done | bytes 294936
  4.0 0.0 copy-start.3
  4.0 1.0 %copy-done.3 = bf16[1,2,6,24,512]{4,3,2,1,0:T(8,128)(2,1)S(1)} copy-done((bf16[1,2,6,24,512]{4,3,2,1,0:T(8,128)(2,1)S(1)}, bf16[1,2,6,24,512]{4,3,2,1,0:T(8,128)(2,1)}, u32[]{:S(2)}) %copy-start.3) | copy-done | bytes 294936
  5.0 0.0 copy-start.4
  5.0 0.9 %copy-done.4 = bf16[320,288]{1,0:T(8,128)(2,1)S(1)} copy-done((bf16[320,288]{1,0:T(8,128)(2,1)S(1)}, bf16[320,288]{1,0:T(8,128)(2,1)}, u32[]{:S(2)}) %copy-start.4) | copy-done | bytes 184344
  6.0 0.0 copy-start.5
  6.0 0.9 %copy-done.5 = bf16[320,288]{1,0:T(8,128)(2,1)S(1)} copy-done((bf16[320,288]{1,0:T(8,128)(2,1)S(1)}, bf16[320,288]{1,0:T(8,128)(2,1)}, u32[]{:S(2)}) %copy-start.5) | copy-done | bytes 184344
  6.9 0.0 copy-start.6
  6.9 0.9 %copy-done.6 = bf16[288,320]{1,0:T(8,128)(2,1)S(1)} copy-done((bf16[288,320]{1,0:T(8,128)(2,1)S(1)}, bf16[288,320]{1,0:T(8,128)(2,1)}, u32[]{:S(2)}) %copy-start.6) | copy-done | bytes 184344
  7.8 0.0 copy-start.7
  7.8 0.9 %copy-done.7 = bf16[288,320]{1,0:T(8,128)(2,1)S(1)} copy-done((bf16[288,320]{1,0:T(8,128)(2,1)S(1)}, bf16[288,320]{1,0:T(8,128)(2,1)}, u32[]{:S(2)}) %copy-start.7) | copy-done | bytes 184344
  8.8 0.0 copy-start.8
  8.8 0.9 %copy-done.8 = f32[288,128]{1,0:T(8,128)S(1)} copy-done((f32[288,128]{1,0:T(8,128)S(1)}, f32[288,128]{1,0:T(8,128)}, u32[]{:S(2)}) %copy-start.8) | copy-done | bytes 147480
  9.7 0.0 copy-start.9
  9.7 0.9 %copy-done.9 = f32[288,24]{1,0:T(8,128)S(1)} copy-done((f32[288,24]{1,0:T(8,128)S(1)}, f32[288,24]{1,0:T(8,128)}, u32[]{:S(2)}) %copy-start.9) | copy-done | bytes 27672
  10.6 0.0 copy-start.10
  10.6 0.9 %copy-done.10 = s32[24,768]{1,0:T(8,128)S(1)} copy-done((s32[24,768]{1,0:T(8,128)S(1)}, s32[24,768]{1,0:T(8,128)}, u32[]{:S(2)}) %copy-start.10) | copy-done | bytes 73752
  11.5 0.0 copy-start.11
  11.5 0.7 %copy-done.11 = f32[1,512]{1,0:T(1,128)S(1)} copy-done((f32[1,512]{1,0:T(1,128)S(1)}, f32[1,512]{1,0:T(1,128)}, u32[]{:S(2)}) %copy-start.11) | copy-done | bytes 2072
  12.2 50.5 %sublayer.1 = (bf16[288,512]{1,0:T(8,128)(2,1)S(1)}, f32[4,512]{1,0:T(4,128)S(1)}) custom-call(bf16[288,512]{1,0:T(8,128)(2,1)S(1)} %bitcast.7, bf16[288,512]{1,0:T(8,128)(2,1)S(1)} %bitcast.8, f32[1,512]{1,0:T(1,128)S(1)} %copy-done.11, bf16[512,1536]{1,0:T(8,128)(2,1)S(1)} %bitcast.5, bf16[512,512]{1,0:T(8,128)(2,1)S(1)} %bitcast.6, ...), custom_call_target="tpu_custom_call" | custom-call | tf_op jit(solution)/shard_map/sublayer/pallas_call | solution.py:381
  62.6 0.7 %copy.16 = bf16[1,2,6,24,512]{4,3,2,1,0:T(8,128)(2,1)} copy(bf16[1,2,6,24,512]{4,3,2,1,0:T(8,128)(2,1)S(1)} %bitcast.9) | data formatting | bytes 589824
  63.3 0.6 copy.17
Async XLA Ops:
  0.6 1.4 %copy-start = (bf16[1,512,1536]{2,1,0:T(8,128)(2,1)S(1)}, bf16[1,512,1536]{2,1,0:T(8,128)(2,1)}, u32[]{:S(2)}) copy-start(bf16[1,512,1536]{2,1,0:T(8,128)(2,1)} %param.15) | copy-start | bytes 4718596
  2.0 1.0 %copy-start.1 = (bf16[1,512,512]{2,1,0:T(8,128)(2,1)S(1)}, bf16[1,512,512]{2,1,0:T(8,128)(2,1)}, u32[]{:S(2)}) copy-start(bf16[1,512,512]{2,1,0:T(8,128)(2,1)} %param.16) | copy-start | bytes 1572868
  3.1 1.0 %copy-start.2 = (bf16[1,2,6,24,512]{4,3,2,1,0:T(8,128)(2,1)S(1)}, bf16[1,2,6,24,512]{4,3,2,1,0:T(8,128)(2,1)}, u32[]{:S(2)}) copy-start(bf16[1,2,6,24,512]{4,3,2,1,0:T(8,128)(2,1)} %param.12) | copy-start | bytes 884740
  4.0 1.0 %copy-start.3 = (bf16[1,2,6,24,512]{4,3,2,1,0:T(8,128)(2,1)S(1)}, bf16[1,2,6,24,512]{4,3,2,1,0:T(8,128)(2,1)}, u32[]{:S(2)}) copy-start(bf16[1,2,6,24,512]{4,3,2,1,0:T(8,128)(2,1)} %param.13) | copy-start | bytes 884740
  5.0 0.9 %copy-start.4 = (bf16[320,288]{1,0:T(8,128)(2,1)S(1)}, bf16[320,288]{1,0:T(8,128)(2,1)}, u32[]{:S(2)}) copy-start(bf16[320,288]{1,0:T(8,128)(2,1)} %constant.14.clone.pret_hbm) | copy-start | bytes 552964
  6.0 0.9 %copy-start.5 = (bf16[320,288]{1,0:T(8,128)(2,1)S(1)}, bf16[320,288]{1,0:T(8,128)(2,1)}, u32[]{:S(2)}) copy-start(bf16[320,288]{1,0:T(8,128)(2,1)} %constant.12.clone.psend_hbm) | copy-start | bytes 552964
  6.9 0.9 %copy-start.6 = (bf16[288,320]{1,0:T(8,128)(2,1)S(1)}, bf16[288,320]{1,0:T(8,128)(2,1)}, u32[]{:S(2)}) copy-start(bf16[288,320]{1,0:T(8,128)(2,1)} %constant.15.clone.pout_hbm) | copy-start | bytes 552964
  7.8 0.9 %copy-start.7 = (bf16[288,320]{1,0:T(8,128)(2,1)S(1)}, bf16[288,320]{1,0:T(8,128)(2,1)}, u32[]{:S(2)}) copy-start(bf16[288,320]{1,0:T(8,128)(2,1)} %constant.13.clone.pwin_hbm) | copy-start | bytes 552964
  8.8 0.9 %copy-start.8 = (f32[288,128]{1,0:T(8,128)S(1)}, f32[288,128]{1,0:T(8,128)}, u32[]{:S(2)}) copy-start(f32[288,128]{1,0:T(8,128)} %constant.17.clone.cols_hbm) | copy-start | bytes 442372
  9.7 0.9 %copy-start.9 = (f32[288,24]{1,0:T(8,128)S(1)}, f32[288,24]{1,0:T(8,128)}, u32[]{:S(2)}) copy-start(f32[288,24]{1,0:T(8,128)} %constant.16.clone.rows_hbm) | copy-start | bytes 82948
  10.6 0.9 %copy-start.10 = (s32[24,768]{1,0:T(8,128)S(1)}, s32[24,768]{1,0:T(8,128)}, u32[]{:S(2)}) copy-start(s32[24,768]{1,0:T(8,128)} %labels_hbm.1) | copy-start | bytes 221188
  11.5 0.7 %copy-start.11 = (f32[1,512]{1,0:T(1,128)S(1)}, f32[1,512]{1,0:T(1,128)}, u32[]{:S(2)}) copy-start(f32[1,512]{1,0:T(1,128)} %gain_hbm.1) | copy-start | bytes 6148

commit v2 on v1

v2 whole, which is shorter than its diff:
```python
import functools

import jax
import jax.numpy as jnp
import numpy as np
from jax import lax
from jax.experimental import pallas as pl
from jax.experimental.pallas import tpu as pltpu
from jax.sharding import PartitionSpec as P

MESH = pl.DeviceIdType.MESH
LEV = 2
LAT_CELLS = 6
LON_CELLS = 24
TOKENS = 288
WIN = 144
D = 512
GROUP = 256
HEADS = 4
COLS = HEADS * WIN
PART_AT = {"00": 0, "10": 112, "01": 224, "11": 272}
PART_ROWS = 320
ACTS_AT = {"own": 0, "10": 288, "01": 400, "11": 448}
ACTS_ROWS = 496
SIZE = {"00": 112, "10": 112, "01": 48, "11": 48}
epsilon = 1e-05
masked_score = -1e30
open_score = 3e38


def natural(lev, row, col):
    return (lev * LAT_CELLS + row) * LON_CELLS + col


def cells(group, part):
    rows = range(0, 3) if group[0] == "1" else range(3, 6)
    if group[1] == "1":
        cols = range(0, 6) if part == 1 else ()
    else:
        cols = range(6, 18) if part == 0 else range(18, 24)
    return [(l, r, c) for l in range(LEV) for r in rows for c in cols]


def layouts():
    groups = ("00", "10", "01", "11")
    place = {g: {cell: n for n, cell in enumerate(cells(g, 0) + cells(g, 1))} for g in groups}

    part = np.zeros((PART_ROWS, TOKENS), np.float32)
    acts_win = np.zeros((TOKENS, ACTS_ROWS), np.float32)
    part_win = np.zeros((TOKENS, PART_ROWS), np.float32)
    rows = np.zeros((TOKENS, 24), np.float32)
    cols = np.zeros((TOKENS, 128), np.float32)
    order = [(g, cell) for w in range(2) for g in groups for cell in cells(g, w)]
    for t, (g, cell) in enumerate(order):
        n = place[g][cell]
        part[PART_AT[g] + n, natural(*cell)] = 1
        part_win[t, PART_AT[g] + n] = 1
        acts_win[t, natural(*cell) if g == "00" else ACTS_AT[g] + n] = 1
        rows[t, cell[1] + (6 if g[0] == "1" else 0)] = 1
        cols[t, cell[2] + (24 if g[1] == "1" else 0)] = 1
    return part, acts_win, part_win, part_win.T, part.T, rows, cols


def regroup(pieces, per):
    old = np.arange(4 * pieces * per).reshape(4, pieces, per).transpose(1, 0, 2).reshape(-1)
    matrix = np.zeros((old.size, old.size), np.float32)
    matrix[np.arange(old.size), old] = 1
    return matrix


def dot(left, right, dims=((1,), (0,))):
    return lax.dot_general(left, right, (dims, ((), ())), preferred_element_type=jnp.float32)


NT = ((1,), (1,))
TN = ((0,), (0,))


def kernel(
    sizes,
    acts_hbm, grads_hbm, gain_hbm, wqkv_hbm, wout_hbm, labels_hbm,
    part_hbm, awin_hbm, gwin_hbm, back_hbm, home_hbm, rows_hbm, cols_hbm, regroup_hbm,
    out_ref, wo_ref,
    acts_buf, grads_v, gain_v, wqkv_v, wout_v, labels_v,
    part_v, awin_v, gwin_v, back_v, home_v, rows_v, cols_v, regroup_v,
    acts_part, grads_part, grads_buf, ret_send, ret_recv,
    mask_v, perm_v, qkv_v, qb_v, w_v, wl_v, att_v, up_v, ga_v, gb_v, gp_v, cen_v, inv_v,
    own_v, a_send, a_recv, b_send, b_recv, c_send, c_recv,
    in_sem, send_sem, recv_sem, ready_sem,
):
    pipe_n, nx, ny, nz = sizes
    lon_n, lat_n = nx * ny, nz * 2
    s = lax.axis_index("pipe")
    j = lax.axis_index("lon")
    i = lax.axis_index("lat")
    x, y = j // ny, j % ny
    z, core = i // 2, i % 2

    def near(ds, dj, di):
        return (
            (s + ds + pipe_n) % pipe_n if ds else s,
            (j + dj + lon_n) % lon_n if dj else j,
            (i + di + lat_n) % lat_n if di else i,
        )

    def on_x(k):
        return (s, ((x + k) % nx) * ny + y, i)

    def on_yz(k):
        return (s, x * ny + (y + k // nz) % ny, (z + k % nz) % nz * 2 + core)

    twin = (s, j, z * 2 + (1 - core))

    barrier = pltpu.get_barrier_semaphore()
    greeted = [near(0, 0, 1), near(0, 1, 0), near(0, 1, 1), near(0, 0, -1), near(0, -1, 0), near(0, -1, -1), twin]
    greeted += [on_x(k) for k in range(1, nx)] + [on_yz(k) for k in range(1, ny * nz)]
    before = [near(-1, 0, 0), near(-1, 0, -1), near(-1, -1, 0), near(-1, -1, -1)]
    after = [near(1, 0, 0), near(1, 0, 1), near(1, 1, 0), near(1, 1, 1)]
    last = pipe_n - 1

    def greet(devices):
        for device in devices:
            pl.semaphore_signal(barrier, inc=1, device_id=device, device_id_type=MESH)

    @pl.when(s != last)
    def _():
        greet(after)

    @pl.when(s == 0)
    def _():
        greet(before)

    greet(greeted)

    loads = []
    for n, (src, dst) in enumerate((
        (acts_hbm, acts_buf.at[pl.ds(0, TOKENS)]), (part_hbm, part_v), (grads_hbm, grads_v), (labels_hbm, labels_v),
        (rows_hbm, rows_v), (cols_hbm, cols_v), (awin_hbm, awin_v), (gain_hbm, gain_v),
        (wqkv_hbm, wqkv_v), (gwin_hbm, gwin_v), (wout_hbm, wout_v), (regroup_hbm, regroup_v),
        (back_hbm, back_v), (home_hbm, home_v),
    )):
        load = pltpu.make_async_copy(src, dst, in_sem.at[n])
        load.start()
        loads.append(load)
    (
        l_acts, l_part, l_grads, l_labels, l_rows, l_cols, l_awin, l_gain,
        l_wqkv, l_gwin, l_wout, l_regroup, l_back, l_home,
    ) = loads

    planned = []

    def plan(src, dst, device):
        n = len(planned)
        copy = pltpu.make_async_remote_copy(
            src_ref=src, dst_ref=dst, send_sem=send_sem.at[n], recv_sem=recv_sem.at[n],
            device_id=device, device_id_type=MESH,
        )
        planned.append(copy)
        return copy

    def send(src, dst, device):
        copy = plan(src, dst, device)
        copy.start()
        return copy

    def block(ref, at, size):
        return ref.at[pl.ds(at, size)]

    here = {"10": (0, -1), "11": (-1, -1), "00": (0, 0), "01": (-1, 0)}
    acts_in = [
        plan(block(acts_part, PART_AT[g] - 112, SIZE[g]), block(acts_buf, ACTS_AT[g], SIZE[g]), near(0, *here[g]))
        for g in ("10", "11", "01")
    ]
    grads_in = [
        plan(block(grads_part, PART_AT[g], SIZE[g]), block(grads_buf, PART_AT[g], SIZE[g]), near(-1, *here[g]))
        for g in ("10", "11", "00", "01")
    ]

    l_acts.wait()
    l_part.wait()
    acts_part[...] = dot(part_v[112:], acts_buf[0:TOKENS]).astype(jnp.bfloat16)
    pl.semaphore_wait(barrier, len(greeted) + jnp.where(s > 0, 4, 0) + jnp.where(s == last, 4, 0))

    @pl.when(s == last)
    def _():
        for device in after:
            pl.semaphore_signal(ready_sem, inc=1, device_id=device, device_id_type=MESH)

    for copy in acts_in:
        copy.start()
    l_grads.wait()
    grads_part[...] = dot(part_v[...], grads_v[...]).astype(jnp.bfloat16)

    @pl.when(s != 0)
    def _():
        for copy in grads_in:
            copy.start()

    l_labels.wait()
    l_rows.wait()
    l_cols.wait()
    row_n, col_n = labels_v.shape
    cell = lax.broadcasted_iota(jnp.int32, (col_n, 128), 0) - j * LON_CELLS
    cell = jnp.where(cell < 0, cell + col_n, cell)
    pick_col = (cell == lax.broadcasted_iota(jnp.int32, (col_n, 128), 1)).astype(jnp.float32)
    row = lax.broadcasted_iota(jnp.int32, (row_n, row_n), 1) - i * LAT_CELLS
    row = jnp.where(row < 0, row + row_n, row)
    pick_row = (row == lax.broadcasted_iota(jnp.int32, (row_n, row_n), 0)).astype(jnp.float32)
    near_labels = dot(pick_row, dot(labels_v[...].astype(jnp.float32), pick_col))
    token_label = jnp.sum(dot(rows_v[...], near_labels) * cols_v[...], -1, keepdims=True)
    lane = lax.broadcasted_iota(jnp.int32, (TOKENS, 128), 1).astype(jnp.float32)
    one_hot = (token_label == lane).astype(jnp.float32).astype(jnp.bfloat16)
    for w in range(2):
        here = one_hot[w * WIN:(w + 1) * WIN]
        alike = dot(here, jnp.concatenate([here] * HEADS, 0), NT)
        mask_v[w] = jnp.where(alike > 0.5, open_score, masked_score)

    per = D // (2 * nx * ny * nz)
    m = lax.broadcasted_iota(jnp.int32, (D, D), 0)
    r_at = m % per
    z_at = (m // per) % nz
    y_at = (m // (per * nz)) % ny
    x_at = (m // (per * nz * ny)) % nx
    c_at = m // (per * nz * ny * nx)
    feature = (
        (((x_at + x) % nx * ny + (y_at + y) % ny) * nz + (z_at + z) % nz) * 2 + (c_at + core) % 2
    ) * per + r_at
    perm_v[...] = (feature == lax.broadcasted_iota(jnp.int32, (D, D), 1)).astype(jnp.float32).astype(jnp.bfloat16)

    l_awin.wait()
    l_gain.wait()
    l_wqkv.wait()
    for copy in acts_in:
        copy.wait_recv()
    gain = gain_v[...]
    inputs = dot(awin_v[...], acts_buf[...])
    mean = jnp.mean(inputs, -1, keepdims=True)
    centred = inputs - mean
    inverse = 1.0 / jnp.sqrt(jnp.mean(centred * centred, -1, keepdims=True) + epsilon)
    centred = centred * inverse
    cen_v[...] = centred
    inv_v[...] = jnp.broadcast_to(inverse, inv_v.shape)
    projected = dot((centred * gain).astype(jnp.bfloat16), wqkv_v[...])
    for part in range(3):
        for w in range(2):
            for g in range(2):
                at = part * D + g * GROUP
                qkv_v[part, w * 2 + g] = projected[w * WIN:(w + 1) * WIN, at:at + GROUP].astype(jnp.bfloat16)

    head_lane = lax.broadcasted_iota(jnp.int32, (1, GROUP), 1) // 64
    head_mask = [(head_lane == h).astype(jnp.float32) for h in range(HEADS)]

    def spread(block, dst, n, scale):
        for h in range(HEADS):
            dst[n, h * WIN:(h + 1) * WIN, :] = (block * (head_mask[h] * scale)).astype(jnp.bfloat16)

    def gather(product):
        total = product[0:WIN] * head_mask[0]
        for h in range(1, HEADS):
            total = total + product[h * WIN:(h + 1) * WIN] * head_mask[h]
        return total

    def forward(n, carry):
        spread(qkv_v[0, n].astype(jnp.float32), qb_v, n, 0.125)
        scores = jnp.minimum(dot(qkv_v[1, n], qb_v[n], NT), mask_v[n // 2])
        exps = jnp.exp(scores - jnp.max(scores, 0, keepdims=True))
        weights = exps * (1.0 / jnp.sum(exps, 0, keepdims=True))
        w_v[n] = weights
        low = weights.astype(jnp.bfloat16)
        wl_v[n] = low
        att_v[n] = gather(dot(low, qkv_v[2, n], TN)).astype(jnp.bfloat16)
        return carry

    @pl.when(s == 0)
    def _():
        pl.semaphore_wait(ready_sem, 4)
        for copy in grads_in:
            copy.start()

    lax.fori_loop(0, 4, forward, 0)

    l_wout.wait()
    l_gwin.wait()
    for copy in grads_in:
        copy.wait_recv()
    upstream = dot(gwin_v[...], grads_buf[...]).astype(jnp.bfloat16)
    up_v[...] = upstream
    attended = jnp.concatenate(
        [jnp.concatenate([att_v[2 * w], att_v[2 * w + 1]], 1) for w in range(2)], 0
    )
    turned = dot(perm_v[...], attended, NT).astype(jnp.bfloat16)
    half = D // 2
    a_send[...] = dot(turned[half:], upstream).astype(jnp.bfloat16)
    step_a = send(a_send, a_recv, twin)
    own_v[...] = dot(turned[:half], upstream)

    grad_att = dot(upstream, wout_v[...], NT)
    for w in range(2):
        for g in range(2):
            ga_v[w * 2 + g] = grad_att[w * WIN:(w + 1) * WIN, g * GROUP:(g + 1) * GROUP].astype(jnp.bfloat16)

    def backward(n, carry):
        spread(ga_v[n].astype(jnp.float32), gb_v, n, 1.0)
        grad_w = dot(qkv_v[2, n], gb_v[n], NT)
        weights = w_v[n]
        inner = jnp.sum(grad_w * weights, 0, keepdims=True)
        grad_s = (weights * (grad_w - inner)).astype(jnp.bfloat16)
        gp_v[0, n] = (gather(dot(grad_s, qkv_v[1, n], TN)) * 0.125).astype(jnp.bfloat16)
        gp_v[1, n] = dot(grad_s, qb_v[n]).astype(jnp.bfloat16)
        gp_v[2, n] = dot(wl_v[n], gb_v[n]).astype(jnp.bfloat16)
        return carry

    lax.fori_loop(0, 2, backward, 0)

    step_a.wait_recv()
    chunk = half // nx
    summed = own_v[...] + a_recv[...].astype(jnp.float32)
    own_v[...] = summed
    b_send[...] = summed.astype(jnp.bfloat16)
    step_b = [
        send(b_send.at[pl.ds(k * chunk, chunk)], b_recv.at[pl.ds((k - 1) * chunk, chunk)], on_x(k))
        for k in range(1, nx)
    ]

    lax.fori_loop(2, 4, backward, 0)

    grad_proj = jnp.concatenate(
        [
            jnp.concatenate([gp_v[part, 2 * w + g] for part in range(3) for g in range(2)], 1)
            for w in range(2)
        ],
        0,
    )
    scaled = dot(grad_proj, wqkv_v[...], NT) * gain
    centred = cen_v[...]
    first = jnp.mean(scaled, -1, keepdims=True)
    second = jnp.mean(scaled * centred, -1, keepdims=True)
    branch = inv_v[:, 0:1] * (scaled - first - centred * second)
    result = (up_v[...].astype(jnp.float32) + branch).astype(jnp.bfloat16)
    for copy in step_b:
        copy.wait_recv()
    total = own_v[0:chunk, :]
    for k in range(1, nx):
        total = total + b_recv[(k - 1) * chunk:k * chunk, :].astype(jnp.float32)
    own_v[0:chunk, :] = total
    l_regroup.wait()
    low = total.astype(jnp.bfloat16)
    stacked = jnp.concatenate([low[:, q * 128:(q + 1) * 128] for q in range(4)], 0)
    c_send[...] = dot(regroup_v[...], stacked).astype(jnp.bfloat16)
    size = 4 * per
    step_c = [
        send(block(c_send, k * size, size), block(c_recv, k * size, size), on_yz(k)) for k in range(1, ny * nz)
    ]

    l_back.wait()
    back = dot(back_v[...], result).astype(jnp.bfloat16)
    ret_send[...] = back
    ret_recv[0:112, :] = back[0:112]
    ret_in = [
        send(block(ret_send, PART_AT[g], SIZE[g]), block(ret_recv, PART_AT[g], SIZE[g]), device)
        for g, device in (("10", near(0, 0, 1)), ("11", near(0, 1, 1)), ("01", near(0, 1, 0)))
    ]

    for copy in step_c:
        copy.wait_recv()
    got = c_recv[size:2 * size].astype(jnp.float32)
    for k in range(2, ny * nz):
        got = got + c_recv[k * size:(k + 1) * size].astype(jnp.float32)
    wo_ref[...] = own_v[0:per, :] + jnp.concatenate([got[q * per:(q + 1) * per] for q in range(4)], 1)

    l_home.wait()
    for copy in ret_in:
        copy.wait_recv()
    out_ref[...] = dot(home_v[...], ret_recv[...]).astype(jnp.bfloat16)
    for copy in planned:
        copy.wait_send()


def on_device(sizes, acts, section_grads, gain, w_qkv, w_out, labels):
    pipe_n, nx, ny, nz = sizes
    per = D // (2 * nx * ny * nz)
    half = D // 2
    chunk = half // nx
    bf, f32 = jnp.bfloat16, jnp.float32
    part, acts_win, part_win, back, home, rows, cols = layouts()
    tables = [jnp.asarray(m, bf) for m in (part, acts_win, part_win, back, home)]
    tables += [jnp.asarray(rows), jnp.asarray(cols), jnp.asarray(regroup(ny * nz, per), bf)]
    sends = 3 + 4 + 3 + 1 + (nx - 1) + (ny * nz - 1)
    vm = pltpu.VMEM
    scratch = [
        vm((ACTS_ROWS, D), bf), vm((TOKENS, D), bf), vm((1, D), f32), vm((D, 3 * D), bf), vm((D, D), bf),
        vm(labels.shape, jnp.int32),
    ]
    scratch += [vm(m.shape, m.dtype) for m in tables]
    scratch += [
        vm((PART_ROWS - 112, D), bf), vm((PART_ROWS, D), bf), vm((PART_ROWS, D), bf), vm((PART_ROWS, D), bf), vm((PART_ROWS, D), bf),
    ]
    scratch += [
        vm((2, WIN, COLS), f32), vm((D, D), bf), vm((3, 4, WIN, GROUP), bf), vm((4, COLS, GROUP), bf),
        vm((4, WIN, COLS), f32), vm((4, WIN, COLS), bf), vm((4, WIN, GROUP), bf), vm((TOKENS, D), bf),
        vm((4, WIN, GROUP), bf), vm((4, COLS, GROUP), bf), vm((3, 4, WIN, GROUP), bf),
        vm((TOKENS, D), f32), vm((TOKENS, 128), f32),
    ]
    scratch += [
        vm((half, D), f32), vm((half, D), bf), vm((half, D), bf), vm((half, D), bf),
        vm((max(nx - 1, 1) * chunk, D), bf), vm((4 * chunk, 128), bf), vm((4 * chunk, 128), bf),
        pltpu.SemaphoreType.DMA((6 + len(tables),)),
        pltpu.SemaphoreType.DMA((sends,)), pltpu.SemaphoreType.DMA((sends,)), pltpu.SemaphoreType.REGULAR,
    ]
    anywhere = pl.BlockSpec(memory_space=pltpu.HBM)
    out, wo = pl.pallas_call(
        functools.partial(kernel, sizes),
        out_shape=(jax.ShapeDtypeStruct((TOKENS, D), bf), jax.ShapeDtypeStruct((per, D), f32)),
        in_specs=[anywhere] * (6 + len(tables)),
        out_specs=(pl.BlockSpec(memory_space=pltpu.VMEM), pl.BlockSpec(memory_space=pltpu.VMEM)),
        scratch_shapes=scratch,
        compiler_params=pltpu.CompilerParams(
            collective_id=0, has_side_effects=True, vmem_limit_bytes=60 * 1024 * 1024
        ),
        name="sublayer",
    )(
        acts.reshape(TOKENS, D), section_grads.reshape(TOKENS, D), gain, w_qkv[0], w_out[0], labels,
        *tables,
    )
    return out.reshape(acts.shape), wo


def solution(mesh):
    pipe_n, lon_n, lat_n = (mesh.shape[axis] for axis in ("pipe", "lon", "lat"))
    ny = 8 if lon_n == 32 else min(lon_n, 2)
    sizes = (pipe_n, lon_n // ny, ny, lat_n // 2)
    in_specs = (
        P("pipe", None, "lat", "lon", None),
        P("pipe", None, "lat", "lon", None),
        P("pipe", None),
        P("pipe", None, None),
        P("pipe", None, None),
        P(),
    )
    out_specs = (P("pipe", None, "lat", "lon", None), P(("pipe", "lon", "lat"), None))
    return jax.shard_map(
        functools.partial(on_device, sizes), mesh=mesh, in_specs=in_specs, out_specs=out_specs, check_vma=False
    )
```

time: 64.4 us -> 51.2 us (0.80)
  local copies, waits for them, and re-layouts: 12.8 us -> 2.99 us
  Pallas kernels: 50.5 us -> 46.7 us
    unnamed x26 -> x2, local copies, waits for them, and re-layouts: 12.8 us -> 2.99 us
    pallas_call x1, Pallas kernels: 50.5 us -> 46.7 us  [on_device(): pl.pallas_call(functools.partial(kernel, sizes), out_shape=(jax.ShapeDtyp...]
where the time goes in v2:
time: 51.2 us; the launch traced here: 50.3 us
  Pallas kernels  46.7 us (91%)
  local copies, waits for them, and re-layouts  2.99 us (6%)
  between operations  0.64 us (1%)
    pallas_call x1, Pallas kernels, on_device(): pl.pallas_call(functools.partial(kernel, sizes), out_shape=(jax.ShapeDtyp...  46.7 us
    unnamed x2, local copies, waits for them, and re-layouts  2.99 us

profile of v2, /device:TPU:1, one launch (start us, length us, event | category | flops | bytes accessed | tf_op | source)
XLA Modules:
  0.0 50.3 jit_solution(15254247939245348842)
XLA Ops:
  0.6 46.7 %sublayer.1 = (bf16[288,512]{1,0:T(8,128)(2,1)}, f32[4,512]{1,0:T(4,128)}) custom-call(bf16[288,512]{1,0:T(8,128)(2,1)} %bitcast.8, bf16[288,512]{1,0:T(8,128)(2,1)} %bitcast.9, f32[1,512]{1,0:T(1,128)} %gain_hbm.1, bf16[512,1536]{1,0:T(8,128)(2,1)} %bitcast.5, bf16[512,512]{1,0:T(8,128)(2,1)} %bitcast.6, s32[24,768]{1,0:T(8,128)} %labels_hbm.1, ...), custom_call_target="tpu_custom_call" | custom-call | tf_op jit(solution)/shard_map/sublayer/pallas_call | solution.py:411
  47.4 1.7 %copy.18 = bf16[1,2,6,24,512]{4,3,2,1,0:T(8,128)(2,1)} copy(bf16[1,2,6,24,512]{4,3,2,1,0:T(8,128)(2,1)} %bitcast.7) | data formatting | bytes 589824
  49.0 1.3 %copy.19 = f32[4,512]{1,0:T(4,128)} copy(f32[4,512]{1,0:T(4,128)} %get-tuple-element.9) | data formatting | bytes 16384

commit v3 on v2

--- a/solution.py
+++ b/solution.py
@@ -45,27 +45,18 @@
     groups = ("00", "10", "01", "11")
     place = {g: {cell: n for n, cell in enumerate(cells(g, 0) + cells(g, 1))} for g in groups}
 
-    part = np.zeros((PART_ROWS, TOKENS), np.float32)
-    acts_win = np.zeros((TOKENS, ACTS_ROWS), np.float32)
-    part_win = np.zeros((TOKENS, PART_ROWS), np.float32)
-    rows = np.zeros((TOKENS, 24), np.float32)
-    cols = np.zeros((TOKENS, 128), np.float32)
+    table = np.full((PART_ROWS, 8), -1, np.int32)
     order = [(g, cell) for w in range(2) for g in groups for cell in cells(g, w)]
     for t, (g, cell) in enumerate(order):
         n = place[g][cell]
-        part[PART_AT[g] + n, natural(*cell)] = 1
-        part_win[t, PART_AT[g] + n] = 1
-        acts_win[t, natural(*cell) if g == "00" else ACTS_AT[g] + n] = 1
-        rows[t, cell[1] + (6 if g[0] == "1" else 0)] = 1
-        cols[t, cell[2] + (24 if g[1] == "1" else 0)] = 1
-    return part, acts_win, part_win, part_win.T, part.T, rows, cols
-
-
-def regroup(pieces, per):
-    old = np.arange(4 * pieces * per).reshape(4, pieces, per).transpose(1, 0, 2).reshape(-1)
-    matrix = np.zeros((old.size, old.size), np.float32)
-    matrix[np.arange(old.size), old] = 1
-    return matrix
+        table[PART_AT[g] + n, 0] = natural(*cell)
+        table[PART_AT[g] + n, 1] = t
+        table[t, 2] = natural(*cell) if g == "00" else ACTS_AT[g] + n
+        table[t, 3] = PART_AT[g] + n
+        table[natural(*cell), 4] = PART_AT[g] + n
+        table[t, 5] = cell[1] + (6 if g[0] == "1" else 0)
+        table[t, 6] = cell[2] + (24 if g[1] == "1" else 0)
+    return table
 
 
 def dot(left, right, dims=((1,), (0,))):
@@ -79,14 +70,15 @@
 def kernel(
     sizes,
     acts_hbm, grads_hbm, gain_hbm, wqkv_hbm, wout_hbm, labels_hbm,
-    part_hbm, awin_hbm, gwin_hbm, back_hbm, home_hbm, rows_hbm, cols_hbm, regroup_hbm,
+    table_hbm,
     out_ref, wo_ref,
     acts_buf, grads_v, gain_v, wqkv_v, wout_v, labels_v,
-    part_v, awin_v, gwin_v, back_v, home_v, rows_v, cols_v, regroup_v,
+    table_v,
+    part_v, awin_v, gwin_v, back_v, home_v, regroup_v,
     acts_part, grads_part, grads_buf, ret_send, ret_recv,
     mask_v, perm_v, qkv_v, qb_v, w_v, wl_v, att_v, up_v, ga_v, gb_v, gp_v, cen_v, inv_v,
     own_v, a_send, a_recv, b_send, b_recv, c_send, c_recv,
-    in_sem, send_sem, recv_sem, ready_sem,
+    in_sem, send_sem, recv_sem, ready_sem, across_sem,
 ):
     pipe_n, nx, ny, nz = sizes
     lon_n, lat_n = nx * ny, nz * 2
@@ -113,7 +105,8 @@
 
     barrier = pltpu.get_barrier_semaphore()
     greeted = [near(0, 0, 1), near(0, 1, 0), near(0, 1, 1), near(0, 0, -1), near(0, -1, 0), near(0, -1, -1), twin]
-    greeted += [on_x(k) for k in range(1, nx)] + [on_yz(k) for k in range(1, ny * nz)]
+    greeted += [on_x(k) for k in range(1, nx)] + [on_yz(k * nz) for k in range(1, ny)]
+    across = [on_yz(k * nz + 1) for k in range(ny)]
     before = [near(-1, 0, 0), near(-1, 0, -1), near(-1, -1, 0), near(-1, -1, -1)]
     after = [near(1, 0, 0), near(1, 0, 1), near(1, 1, 0), near(1, 1, 1)]
     last = pipe_n - 1
@@ -122,6 +115,8 @@
         for device in devices:
             pl.semaphore_signal(barrier, inc=1, device_id=device, device_id_type=MESH)
 
+    greet(greeted)
+
     @pl.when(s != last)
     def _():
         greet(after)
@@ -130,22 +125,24 @@
     def _():
         greet(before)
 
-    greet(greeted)
+    @pl.when(z == 0)
+    def _():
+        greet(across)
+
 
     loads = []
     for n, (src, dst) in enumerate((
-        (acts_hbm, acts_buf.at[pl.ds(0, TOKENS)]), (part_hbm, part_v), (grads_hbm, grads_v), (labels_hbm, labels_v),
-        (rows_hbm, rows_v), (cols_hbm, cols_v), (awin_hbm, awin_v), (gain_hbm, gain_v),
-        (wqkv_hbm, wqkv_v), (gwin_hbm, gwin_v), (wout_hbm, wout_v), (regroup_hbm, regroup_v),
-        (back_hbm, back_v), (home_hbm, home_v),
+        (table_hbm, table_v), (acts_hbm, acts_buf.at[pl.ds(0, TOKENS)]), (grads_hbm, grads_v), (labels_hbm, labels_v),
+        (gain_hbm, gain_v), (wqkv_hbm, wqkv_v), (wout_hbm, wout_v),
     )):
         load = pltpu.make_async_copy(src, dst, in_sem.at[n])
         load.start()
         loads.append(load)
-    (
-        l_acts, l_part, l_grads, l_labels, l_rows, l_cols, l_awin, l_gain,
-        l_wqkv, l_gwin, l_wout, l_regroup, l_back, l_home,
-    ) = loads
+    l_table, l_acts, l_grads, l_labels, l_gain, l_wqkv, l_wout = loads
+
+    def picks(column, rows, cols):
+        found = table_v[0:rows, column:column + 1] == lax.broadcasted_iota(jnp.int32, (rows, cols), 1)
+        return found.astype(jnp.float32)
 
     planned = []
 
@@ -176,15 +173,21 @@
         for g in ("10", "11", "00", "01")
     ]
 
+    l_table.wait()
+    part_v[...] = picks(0, PART_ROWS, TOKENS).astype(jnp.bfloat16)
     l_acts.wait()
-    l_part.wait()
     acts_part[...] = dot(part_v[112:], acts_buf[0:TOKENS]).astype(jnp.bfloat16)
-    pl.semaphore_wait(barrier, len(greeted) + jnp.where(s > 0, 4, 0) + jnp.where(s == last, 4, 0))
+    pl.semaphore_wait(barrier, len(greeted) + jnp.where(s > 0, 4, 0) + jnp.where(s == last, 4, 0) + jnp.where(z > 0, ny, 0))
 
     @pl.when(s == last)
     def _():
         for device in after:
             pl.semaphore_signal(ready_sem, inc=1, device_id=device, device_id_type=MESH)
+
+    @pl.when(z > 0)
+    def _():
+        for device in across:
+            pl.semaphore_signal(across_sem, inc=1, device_id=device, device_id_type=MESH)
 
     for copy in acts_in:
         copy.start()
@@ -197,8 +200,6 @@
             copy.start()
 
     l_labels.wait()
-    l_rows.wait()
-    l_cols.wait()
     row_n, col_n = labels_v.shape
     cell = lax.broadcasted_iota(jnp.int32, (col_n, 128), 0) - j * LON_CELLS
     cell = jnp.where(cell < 0, cell + col_n, cell)
@@ -207,7 +208,7 @@
     row = jnp.where(row < 0, row + row_n, row)
     pick_row = (row == lax.broadcasted_iota(jnp.int32, (row_n, row_n), 0)).astype(jnp.float32)
     near_labels = dot(pick_row, dot(labels_v[...].astype(jnp.float32), pick_col))
-    token_label = jnp.sum(dot(rows_v[...], near_labels) * cols_v[...], -1, keepdims=True)
+    token_label = jnp.sum(dot(picks(5, TOKENS, row_n), near_labels) * picks(6, TOKENS, 128), -1, keepdims=True)
     lane = lax.broadcasted_iota(jnp.int32, (TOKENS, 128), 1).astype(jnp.float32)
     one_hot = (token_label == lane).astype(jnp.float32).astype(jnp.bfloat16)
     for w in range(2):
@@ -227,7 +228,15 @@
     ) * per + r_at
     perm_v[...] = (feature == lax.broadcasted_iota(jnp.int32, (D, D), 1)).astype(jnp.float32).astype(jnp.bfloat16)
 
-    l_awin.wait()
+    awin_v[...] = picks(2, TOKENS, ACTS_ROWS).astype(jnp.bfloat16)
+    gwin_v[...] = picks(3, TOKENS, PART_ROWS).astype(jnp.bfloat16)
+    back_v[...] = picks(1, PART_ROWS, TOKENS).astype(jnp.bfloat16)
+    home_v[...] = picks(4, TOKENS, PART_ROWS).astype(jnp.bfloat16)
+    pieces = ny * nz
+    m = lax.broadcasted_iota(jnp.int32, regroup_v.shape, 0)
+    old = (m // per) % 4 * (pieces * per) + m // (4 * per) * per + m % per
+    regroup_v[...] = (old == lax.broadcasted_iota(jnp.int32, regroup_v.shape, 1)).astype(jnp.float32).astype(jnp.bfloat16)
+
     l_gain.wait()
     l_wqkv.wait()
     for copy in acts_in:
@@ -277,23 +286,24 @@
         for copy in grads_in:
             copy.start()
 
-    lax.fori_loop(0, 4, forward, 0)
-
-    l_wout.wait()
-    l_gwin.wait()
-    for copy in grads_in:
-        copy.wait_recv()
-    upstream = dot(gwin_v[...], grads_buf[...]).astype(jnp.bfloat16)
-    up_v[...] = upstream
+    lax.fori_loop(0, 4, forward, 0, unroll=True)
+
     attended = jnp.concatenate(
         [jnp.concatenate([att_v[2 * w], att_v[2 * w + 1]], 1) for w in range(2)], 0
     )
+    attended = dot(back_v[...], attended).astype(jnp.bfloat16)
     turned = dot(perm_v[...], attended, NT).astype(jnp.bfloat16)
     half = D // 2
-    a_send[...] = dot(turned[half:], upstream).astype(jnp.bfloat16)
+    for copy in grads_in:
+        copy.wait_recv()
+    arrived = grads_buf[...]
+    a_send[...] = dot(turned[half:], arrived).astype(jnp.bfloat16)
     step_a = send(a_send, a_recv, twin)
-    own_v[...] = dot(turned[:half], upstream)
-
+    own_v[...] = dot(turned[:half], arrived)
+
+    upstream = dot(gwin_v[...], arrived).astype(jnp.bfloat16)
+    up_v[...] = upstream
+    l_wout.wait()
     grad_att = dot(upstream, wout_v[...], NT)
     for w in range(2):
         for g in range(2):
@@ -310,7 +320,7 @@
         gp_v[2, n] = dot(wl_v[n], gb_v[n]).astype(jnp.bfloat16)
         return carry
 
-    lax.fori_loop(0, 2, backward, 0)
+    lax.fori_loop(0, 2, backward, 0, unroll=True)
 
     step_a.wait_recv()
     chunk = half // nx
@@ -322,7 +332,7 @@
         for k in range(1, nx)
     ]
 
-    lax.fori_loop(2, 4, backward, 0)
+    lax.fori_loop(2, 4, backward, 0, unroll=True)
 
     grad_proj = jnp.concatenate(
         [
@@ -343,16 +353,20 @@
     for k in range(1, nx):
         total = total + b_recv[(k - 1) * chunk:k * chunk, :].astype(jnp.float32)
     own_v[0:chunk, :] = total
-    l_regroup.wait()
     low = total.astype(jnp.bfloat16)
     stacked = jnp.concatenate([low[:, q * 128:(q + 1) * 128] for q in range(4)], 0)
     c_send[...] = dot(regroup_v[...], stacked).astype(jnp.bfloat16)
     size = 4 * per
+
+    @pl.when(z == 0)
+    def _():
+        pl.semaphore_wait(across_sem, ny)
+
     step_c = [
-        send(block(c_send, k * size, size), block(c_recv, k * size, size), on_yz(k)) for k in range(1, ny * nz)
-    ]
-
-    l_back.wait()
+        send(block(c_send, k * size, size), block(c_recv, k * size, size), on_yz(k))
+        for k in sorted(range(1, pieces), key=lambda k: -min(k // nz, ny - k // nz) - 4 * (k % nz))
+    ]
+
     back = dot(back_v[...], result).astype(jnp.bfloat16)
     ret_send[...] = back
     ret_recv[0:112, :] = back[0:112]
@@ -364,11 +378,10 @@
     for copy in step_c:
         copy.wait_recv()
     got = c_recv[size:2 * size].astype(jnp.float32)
-    for k in range(2, ny * nz):
+    for k in range(2, pieces):
         got = got + c_recv[k * size:(k + 1) * size].astype(jnp.float32)
     wo_ref[...] = own_v[0:per, :] + jnp.concatenate([got[q * per:(q + 1) * per] for q in range(4)], 1)
 
-    l_home.wait()
     for copy in ret_in:
         copy.wait_recv()
     out_ref[...] = dot(home_v[...], ret_recv[...]).astype(jnp.bfloat16)
@@ -382,16 +395,17 @@
     half = D // 2
     chunk = half // nx
     bf, f32 = jnp.bfloat16, jnp.float32
-    part, acts_win, part_win, back, home, rows, cols = layouts()
-    tables = [jnp.asarray(m, bf) for m in (part, acts_win, part_win, back, home)]
-    tables += [jnp.asarray(rows), jnp.asarray(cols), jnp.asarray(regroup(ny * nz, per), bf)]
+    table = layouts()
     sends = 3 + 4 + 3 + 1 + (nx - 1) + (ny * nz - 1)
     vm = pltpu.VMEM
     scratch = [
         vm((ACTS_ROWS, D), bf), vm((TOKENS, D), bf), vm((1, D), f32), vm((D, 3 * D), bf), vm((D, D), bf),
         vm(labels.shape, jnp.int32),
     ]
-    scratch += [vm(m.shape, m.dtype) for m in tables]
+    scratch += [
+        vm(table.shape, jnp.int32), vm((PART_ROWS, TOKENS), bf), vm((TOKENS, ACTS_ROWS), bf), vm((TOKENS, PART_ROWS), bf),
+        vm((PART_ROWS, TOKENS), bf), vm((TOKENS, PART_ROWS), bf), vm((4 * chunk, 4 * chunk), bf),
+    ]
     scratch += [
         vm((PART_ROWS - 112, D), bf), vm((PART_ROWS, D), bf), vm((PART_ROWS, D), bf), vm((PART_ROWS, D), bf), vm((PART_ROWS, D), bf),
     ]
@@ -404,14 +418,15 @@
     scratch += [
         vm((half, D), f32), vm((half, D), bf), vm((half, D), bf), vm((half, D), bf),
         vm((max(nx - 1, 1) * chunk, D), bf), vm((4 * chunk, 128), bf), vm((4 * chunk, 128), bf),
-        pltpu.SemaphoreType.DMA((6 + len(tables),)),
+        pltpu.SemaphoreType.DMA((7,)),
         pltpu.SemaphoreType.DMA((sends,)), pltpu.SemaphoreType.DMA((sends,)), pltpu.SemaphoreType.REGULAR,
+        pltpu.SemaphoreType.REGULAR,
     ]
     anywhere = pl.BlockSpec(memory_space=pltpu.HBM)
     out, wo = pl.pallas_call(
         functools.partial(kernel, sizes),
-        out_shape=(jax.ShapeDtypeStruct((TOKENS, D), bf), jax.ShapeDtypeStruct((per, D), f32)),
-        in_specs=[anywhere] * (6 + len(tables)),
+        out_shape=(pltpu.VMEM((TOKENS, D), bf), pltpu.VMEM((per, D), f32)),
+        in_specs=[anywhere] * 7,
         out_specs=(pl.BlockSpec(memory_space=pltpu.VMEM), pl.BlockSpec(memory_space=pltpu.VMEM)),
         scratch_shapes=scratch,
         compiler_params=pltpu.CompilerParams(
@@ -420,7 +435,7 @@
         name="sublayer",
     )(
         acts.reshape(TOKENS, D), section_grads.reshape(TOKENS, D), gain, w_qkv[0], w_out[0], labels,
-        *tables,
+        jnp.asarray(table),
     )
     return out.reshape(acts.shape), wo
 

time: 51.2 us -> 45.6 us (0.89)
  the two profiles are of different devices: /device:TPU:1 before, /device:TPU:194 now
where the time goes in v3:
time: 45.6 us; the launch traced here: 45.5 us
  Pallas kernels  43.5 us (95%)
  local copies, waits for them, and re-layouts  1.31 us (3%)
  between operations  0.64 us (1%)
    pallas_call x1, Pallas kernels, on_device(): pl.pallas_call(functools.partial(kernel, sizes), out_shape=(pltpu.VMEM((T...  43.5 us
    unnamed x2, local copies, waits for them, and re-layouts  1.31 us

profile of v3, /device:TPU:194, one launch (start us, length us, event | category | flops | bytes accessed | tf_op | source)
XLA Modules:
  0.0 45.5 jit_solution(3553973383698652415)
XLA Ops:
  0.6 43.5 %sublayer.1 = (bf16[288,512]{1,0:T(8,128)(2,1)S(1)}, f32[4,512]{1,0:T(4,128)S(1)}) custom-call(bf16[288,512]{1,0:T(8,128)(2,1)} %bitcast.8, bf16[288,512]{1,0:T(8,128)(2,1)} %bitcast.9, f32[1,512]{1,0:T(1,128)} %gain_hbm.1, bf16[512,1536]{1,0:T(8,128)(2,1)} %bitcast.6, bf16[512,512]{1,0:T(8,128)(2,1)} %bitcast.7, s32[24,768]{1,0:T(8,128)} %labels_hbm.1, ...), custom_call_target="tpu_custom_call" | custom-call | tf_op jit(solution)/shard_map/sublayer/pallas_call | solution.py:426
  44.2 0.7 %copy.11 = bf16[1,2,6,24,512]{4,3,2,1,0:T(8,128)(2,1)} copy(bf16[1,2,6,24,512]{4,3,2,1,0:T(8,128)(2,1)S(1)} %bitcast.5) | data formatting | bytes 589824
  44.9 0.6 %copy.12 = f32[4,512]{1,0:T(4,128)} copy(f32[4,512]{1,0:T(4,128)S(1)} %get-tuple-element.7) | data formatting | bytes 16384

commit v4 on v3

--- a/solution.py
+++ b/solution.py
@@ -103,33 +103,6 @@
 
     twin = (s, j, z * 2 + (1 - core))
 
-    barrier = pltpu.get_barrier_semaphore()
-    greeted = [near(0, 0, 1), near(0, 1, 0), near(0, 1, 1), near(0, 0, -1), near(0, -1, 0), near(0, -1, -1), twin]
-    greeted += [on_x(k) for k in range(1, nx)] + [on_yz(k * nz) for k in range(1, ny)]
-    across = [on_yz(k * nz + 1) for k in range(ny)]
-    before = [near(-1, 0, 0), near(-1, 0, -1), near(-1, -1, 0), near(-1, -1, -1)]
-    after = [near(1, 0, 0), near(1, 0, 1), near(1, 1, 0), near(1, 1, 1)]
-    last = pipe_n - 1
-
-    def greet(devices):
-        for device in devices:
-            pl.semaphore_signal(barrier, inc=1, device_id=device, device_id_type=MESH)
-
-    greet(greeted)
-
-    @pl.when(s != last)
-    def _():
-        greet(after)
-
-    @pl.when(s == 0)
-    def _():
-        greet(before)
-
-    @pl.when(z == 0)
-    def _():
-        greet(across)
-
-
     loads = []
     for n, (src, dst) in enumerate((
         (table_hbm, table_v), (acts_hbm, acts_buf.at[pl.ds(0, TOKENS)]), (grads_hbm, grads_v), (labels_hbm, labels_v),
@@ -140,6 +113,33 @@
         loads.append(load)
     l_table, l_acts, l_grads, l_labels, l_gain, l_wqkv, l_wout = loads
 
+    barrier = pltpu.get_barrier_semaphore()
+    greeted = [near(0, 0, 1), near(0, 1, 1), near(0, 0, -1), near(0, -1, -1), near(0, 1, 0), near(0, -1, 0), twin]
+    greeted += [on_x(k) for k in range(1, nx)] + [on_yz(k * nz) for k in range(1, ny)]
+    across = [on_yz(k * nz + 1) for k in range(ny)]
+    before = [near(-1, 0, 0), near(-1, 0, -1), near(-1, -1, 0), near(-1, -1, -1)]
+    after = [near(1, 0, 0), near(1, 0, 1), near(1, 1, 0), near(1, 1, 1)]
+    last = pipe_n - 1
+
+    def greet(devices):
+        for device in devices:
+            pl.semaphore_signal(barrier, inc=1, device_id=device, device_id_type=MESH)
+
+    greet(greeted)
+
+    @pl.when(s != last)
+    def _():
+        greet(after)
+
+    @pl.when(s == 0)
+    def _():
+        greet(before)
+
+    @pl.when(z == 0)
+    def _():
+        greet(across)
+
+
     def picks(column, rows, cols):
         found = table_v[0:rows, column:column + 1] == lax.broadcasted_iota(jnp.int32, (rows, cols), 1)
         return found.astype(jnp.float32)
@@ -177,6 +177,8 @@
     part_v[...] = picks(0, PART_ROWS, TOKENS).astype(jnp.bfloat16)
     l_acts.wait()
     acts_part[...] = dot(part_v[112:], acts_buf[0:TOKENS]).astype(jnp.bfloat16)
+    l_grads.wait()
+    grads_part[...] = dot(part_v[...], grads_v[...]).astype(jnp.bfloat16)
     pl.semaphore_wait(barrier, len(greeted) + jnp.where(s > 0, 4, 0) + jnp.where(s == last, 4, 0) + jnp.where(z > 0, ny, 0))
 
     @pl.when(s == last)
@@ -191,8 +193,6 @@
 
     for copy in acts_in:
         copy.start()
-    l_grads.wait()
-    grads_part[...] = dot(part_v[...], grads_v[...]).astype(jnp.bfloat16)
 
     @pl.when(s != 0)
     def _():
@@ -320,7 +320,7 @@
         gp_v[2, n] = dot(wl_v[n], gb_v[n]).astype(jnp.bfloat16)
         return carry
 
-    lax.fori_loop(0, 2, backward, 0, unroll=True)
+    lax.fori_loop(0, 1, backward, 0, unroll=True)
 
     step_a.wait_recv()
     chunk = half // nx
@@ -329,10 +329,10 @@
     b_send[...] = summed.astype(jnp.bfloat16)
     step_b = [
         send(b_send.at[pl.ds(k * chunk, chunk)], b_recv.at[pl.ds((k - 1) * chunk, chunk)], on_x(k))
-        for k in range(1, nx)
-    ]
-
-    lax.fori_loop(2, 4, backward, 0, unroll=True)
+        for k in sorted(range(1, nx), key=lambda k: -min(k, nx - k))
+    ]
+
+    lax.fori_loop(1, 4, backward, 0, unroll=True)
 
     grad_proj = jnp.concatenate(
         [
@@ -347,6 +347,14 @@
     second = jnp.mean(scaled * centred, -1, keepdims=True)
     branch = inv_v[:, 0:1] * (scaled - first - centred * second)
     result = (up_v[...].astype(jnp.float32) + branch).astype(jnp.bfloat16)
+    back = dot(back_v[...], result).astype(jnp.bfloat16)
+    ret_send[...] = back
+    ret_recv[0:112, :] = back[0:112]
+    ret_in = [
+        send(block(ret_send, PART_AT[g], SIZE[g]), block(ret_recv, PART_AT[g], SIZE[g]), device)
+        for g, device in (("10", near(0, 0, 1)), ("11", near(0, 1, 1)), ("01", near(0, 1, 0)))
+    ]
+
     for copy in step_b:
         copy.wait_recv()
     total = own_v[0:chunk, :]
@@ -367,14 +375,9 @@
         for k in sorted(range(1, pieces), key=lambda k: -min(k // nz, ny - k // nz) - 4 * (k % nz))
     ]
 
-    back = dot(back_v[...], result).astype(jnp.bfloat16)
-    ret_send[...] = back
-    ret_recv[0:112, :] = back[0:112]
-    ret_in = [
-        send(block(ret_send, PART_AT[g], SIZE[g]), block(ret_recv, PART_AT[g], SIZE[g]), device)
-        for g, device in (("10", near(0, 0, 1)), ("11", near(0, 1, 1)), ("01", near(0, 1, 0)))
-    ]
-
+    for copy in ret_in:
+        copy.wait_recv()
+    out_ref[...] = dot(home_v[...], ret_recv[...]).astype(jnp.bfloat16)
     for copy in step_c:
         copy.wait_recv()
     got = c_recv[size:2 * size].astype(jnp.float32)
@@ -382,9 +385,6 @@
         got = got + c_recv[k * size:(k + 1) * size].astype(jnp.float32)
     wo_ref[...] = own_v[0:per, :] + jnp.concatenate([got[q * per:(q + 1) * per] for q in range(4)], 1)
 
-    for copy in ret_in:
-        copy.wait_recv()
-    out_ref[...] = dot(home_v[...], ret_recv[...]).astype(jnp.bfloat16)
     for copy in planned:
         copy.wait_send()
 

time: 45.6 us -> 44.5 us (0.976)
  the two profiles are of different devices: /device:TPU:194 before, /device:TPU:128 now
where the time goes in v4:
time: 44.5 us; the launch traced here: 44.4 us
  Pallas kernels  42.4 us (95%)
  local copies, waits for them, and re-layouts  1.31 us (3%)
  between operations  0.64 us (1%)
    pallas_call x1, Pallas kernels, on_device(): pl.pallas_call(functools.partial(kernel, sizes), out_shape=(pltpu.VMEM((T...  42.4 us
    unnamed x2, local copies, waits for them, and re-layouts  1.31 us

profile of v4, /device:TPU:128, one launch (start us, length us, event | category | flops | bytes accessed | tf_op | source)
XLA Modules:
  0.0 44.4 jit_solution(14753938831624011799)
XLA Ops:
  0.6 42.4 %sublayer.1 = (bf16[288,512]{1,0:T(8,128)(2,1)S(1)}, f32[4,512]{1,0:T(4,128)S(1)}) custom-call(bf16[288,512]{1,0:T(8,128)(2,1)} %bitcast.8, bf16[288,512]{1,0:T(8,128)(2,1)} %bitcast.9, f32[1,512]{1,0:T(1,128)} %gain_hbm.1, bf16[512,1536]{1,0:T(8,128)(2,1)} %bitcast.6, bf16[512,512]{1,0:T(8,128)(2,1)} %bitcast.7, s32[24,768]{1,0:T(8,128)} %labels_hbm.1, ...), custom_call_target="tpu_custom_call" | custom-call | tf_op jit(solution)/shard_map/sublayer/pallas_call | solution.py:426
  43.0 0.7 %copy.11 = bf16[1,2,6,24,512]{4,3,2,1,0:T(8,128)(2,1)} copy(bf16[1,2,6,24,512]{4,3,2,1,0:T(8,128)(2,1)S(1)} %bitcast.5) | data formatting | bytes 589824
  43.8 0.6 %copy.12 = f32[4,512]{1,0:T(4,128)} copy(f32[4,512]{1,0:T(4,128)S(1)} %get-tuple-element.7) | data formatting | bytes 16384

commit v5 on v4

--- a/solution.py
+++ b/solution.py
@@ -237,6 +237,12 @@
     old = (m // per) % 4 * (pieces * per) + m // (4 * per) * per + m % per
     regroup_v[...] = (old == lax.broadcasted_iota(jnp.int32, regroup_v.shape, 1)).astype(jnp.float32).astype(jnp.bfloat16)
 
+    @pl.when((s == 0) & (core == 1) & (z == 0))
+    def _():
+        pl.semaphore_wait(ready_sem, 4)
+        for copy in grads_in:
+            copy.start()
+
     l_gain.wait()
     l_wqkv.wait()
     for copy in acts_in:
@@ -280,7 +286,7 @@
         att_v[n] = gather(dot(low, qkv_v[2, n], TN)).astype(jnp.bfloat16)
         return carry
 
-    @pl.when(s == 0)
+    @pl.when((s == 0) & ((core == 0) | (z > 0)))
     def _():
         pl.semaphore_wait(ready_sem, 4)
         for copy in grads_in:

time: 44.5 us -> 44.4 us (level)
  the two profiles are of different devices: /device:TPU:128 before, /device:TPU:1 now
where the time goes in v5:
time: 44.4 us; the launch traced here: 44 us
  Pallas kernels  42.1 us (95%)
  local copies, waits for them, and re-layouts  1.31 us (3%)
  between operations  0.64 us (1%)
    pallas_call x1, Pallas kernels, on_device(): pl.pallas_call(functools.partial(kernel, sizes), out_shape=(pltpu.VMEM((T...  42.1 us
    unnamed x2, local copies, waits for them, and re-layouts  1.31 us

profile of v5, /device:TPU:1, one launch (start us, length us, event | category | flops | bytes accessed | tf_op | source)
XLA Modules:
  0.0 44.0 jit_solution(5097656295508090943)
XLA Ops:
  0.6 42.1 %sublayer.1 = (bf16[288,512]{1,0:T(8,128)(2,1)S(1)}, f32[4,512]{1,0:T(4,128)S(1)}) custom-call(bf16[288,512]{1,0:T(8,128)(2,1)} %bitcast.8, bf16[288,512]{1,0:T(8,128)(2,1)} %bitcast.9, f32[1,512]{1,0:T(1,128)} %gain_hbm.1, bf16[512,1536]{1,0:T(8,128)(2,1)} %bitcast.6, bf16[512,512]{1,0:T(8,128)(2,1)} %bitcast.7, s32[24,768]{1,0:T(8,128)} %labels_hbm.1, ...), custom_call_target="tpu_custom_call" | custom-call | tf_op jit(solution)/shard_map/sublayer/pallas_call | solution.py:432
  42.7 0.7 %copy.11 = bf16[1,2,6,24,512]{4,3,2,1,0:T(8,128)(2,1)} copy(bf16[1,2,6,24,512]{4,3,2,1,0:T(8,128)(2,1)S(1)} %bitcast.5) | data formatting | bytes 589824
  43.4 0.6 %copy.12 = f32[4,512]{1,0:T(4,128)} copy(f32[4,512]{1,0:T(4,128)S(1)} %get-tuple-element.7) | data formatting | bytes 16384

commit v6 on v4

--- a/solution.py
+++ b/solution.py
@@ -261,7 +261,7 @@
 
     def spread(block, dst, n, scale):
         for h in range(HEADS):
-            dst[n, h * WIN:(h + 1) * WIN, :] = (block * (head_mask[h] * scale)).astype(jnp.bfloat16)
+            dst[n, h * WIN:(h + 1) * WIN, :] = block * (head_mask[h] * scale).astype(jnp.bfloat16)
 
     def gather(product):
         total = product[0:WIN] * head_mask[0]
@@ -270,7 +270,7 @@
         return total
 
     def forward(n, carry):
-        spread(qkv_v[0, n].astype(jnp.float32), qb_v, n, 0.125)
+        spread(qkv_v[0, n], qb_v, n, 0.125)
         scores = jnp.minimum(dot(qkv_v[1, n], qb_v[n], NT), mask_v[n // 2])
         exps = jnp.exp(scores - jnp.max(scores, 0, keepdims=True))
         weights = exps * (1.0 / jnp.sum(exps, 0, keepdims=True))
@@ -297,8 +297,11 @@
     for copy in grads_in:
         copy.wait_recv()
     arrived = grads_buf[...]
-    a_send[...] = dot(turned[half:], arrived).astype(jnp.bfloat16)
-    step_a = send(a_send, a_recv, twin)
+    quarter = half // 2
+    step_a = []
+    for at in (0, quarter):
+        a_send[at:at + quarter, :] = dot(turned[half + at:half + at + quarter], arrived).astype(jnp.bfloat16)
+        step_a.append(send(block(a_send, at, quarter), block(a_recv, at, quarter), twin))
     own_v[...] = dot(turned[:half], arrived)
 
     upstream = dot(gwin_v[...], arrived).astype(jnp.bfloat16)
@@ -310,7 +313,7 @@
             ga_v[w * 2 + g] = grad_att[w * WIN:(w + 1) * WIN, g * GROUP:(g + 1) * GROUP].astype(jnp.bfloat16)
 
     def backward(n, carry):
-        spread(ga_v[n].astype(jnp.float32), gb_v, n, 1.0)
+        spread(ga_v[n], gb_v, n, 1.0)
         grad_w = dot(qkv_v[2, n], gb_v[n], NT)
         weights = w_v[n]
         inner = jnp.sum(grad_w * weights, 0, keepdims=True)
@@ -322,15 +325,18 @@
 
     lax.fori_loop(0, 1, backward, 0, unroll=True)
 
-    step_a.wait_recv()
+    for copy in step_a:
+        copy.wait_recv()
     chunk = half // nx
-    summed = own_v[...] + a_recv[...].astype(jnp.float32)
-    own_v[...] = summed
-    b_send[...] = summed.astype(jnp.bfloat16)
-    step_b = [
-        send(b_send.at[pl.ds(k * chunk, chunk)], b_recv.at[pl.ds((k - 1) * chunk, chunk)], on_x(k))
-        for k in sorted(range(1, nx), key=lambda k: -min(k, nx - k))
-    ]
+    step_b = []
+    for k in sorted(range(nx), key=lambda k: (k == 0, -min(k, nx - k))):
+        rows = slice(k * chunk, (k + 1) * chunk)
+        summed = own_v[rows, :] + a_recv[rows, :].astype(jnp.float32)
+        if k == 0:
+            own_v[rows, :] = summed
+        else:
+            b_send[rows, :] = summed.astype(jnp.bfloat16)
+            step_b.append(send(block(b_send, k * chunk, chunk), block(b_recv, (k - 1) * chunk, chunk), on_x(k)))
 
     lax.fori_loop(1, 4, backward, 0, unroll=True)
 
@@ -347,13 +353,12 @@
     second = jnp.mean(scaled * centred, -1, keepdims=True)
     branch = inv_v[:, 0:1] * (scaled - first - centred * second)
     result = (up_v[...].astype(jnp.float32) + branch).astype(jnp.bfloat16)
-    back = dot(back_v[...], result).astype(jnp.bfloat16)
-    ret_send[...] = back
-    ret_recv[0:112, :] = back[0:112]
-    ret_in = [
-        send(block(ret_send, PART_AT[g], SIZE[g]), block(ret_recv, PART_AT[g], SIZE[g]), device)
-        for g, device in (("10", near(0, 0, 1)), ("11", near(0, 1, 1)), ("01", near(0, 1, 0)))
-    ]
+    ret_in = []
+    for g, device in (("10", near(0, 0, 1)), ("11", near(0, 1, 1)), ("01", near(0, 1, 0))):
+        rows = slice(PART_AT[g], PART_AT[g] + SIZE[g])
+        ret_send[rows, :] = dot(back_v[rows, :], result).astype(jnp.bfloat16)
+        ret_in.append(send(block(ret_send, PART_AT[g], SIZE[g]), block(ret_recv, PART_AT[g], SIZE[g]), device))
+    ret_recv[0:112, :] = dot(back_v[0:112, :], result).astype(jnp.bfloat16)
 
     for copy in step_b:
         copy.wait_recv()
@@ -396,7 +401,7 @@
     chunk = half // nx
     bf, f32 = jnp.bfloat16, jnp.float32
     table = layouts()
-    sends = 3 + 4 + 3 + 1 + (nx - 1) + (ny * nz - 1)
+    sends = 3 + 4 + 3 + 2 + (nx - 1) + (ny * nz - 1)
     vm = pltpu.VMEM
     scratch = [
         vm((ACTS_ROWS, D), bf), vm((TOKENS, D), bf), vm((1, D), f32), vm((D, 3 * D), bf), vm((D, D), bf),

time: 44.5 us -> 44.5 us (level)
  no operation moved by 1% of the time
where the time goes in v6:
time: 44.5 us; the launch traced here: 44.3 us
  Pallas kernels  42.4 us (95%)
  local copies, waits for them, and re-layouts  1.31 us (3%)
  between operations  0.64 us (1%)
    pallas_call x1, Pallas kernels, on_device(): pl.pallas_call(functools.partial(kernel, sizes), out_shape=(pltpu.VMEM((T...  42.4 us
    unnamed x2, local copies, waits for them, and re-layouts  1.31 us

profile of v6, /device:TPU:128, one launch (start us, length us, event | category | flops | bytes accessed | tf_op | source)
XLA Modules:
  0.0 44.3 jit_solution(15541969895387740095)
XLA Ops:
  0.6 42.4 %sublayer.1 = (bf16[288,512]{1,0:T(8,128)(2,1)S(1)}, f32[4,512]{1,0:T(4,128)S(1)}) custom-call(bf16[288,512]{1,0:T(8,128)(2,1)} %bitcast.8, bf16[288,512]{1,0:T(8,128)(2,1)} %bitcast.9, f32[1,512]{1,0:T(1,128)} %gain_hbm.1, bf16[512,1536]{1,0:T(8,128)(2,1)} %bitcast.6, bf16[512,512]{1,0:T(8,128)(2,1)} %bitcast.7, s32[24,768]{1,0:T(8,128)} %labels_hbm.1, ...), custom_call_target="tpu_custom_call" | custom-call | tf_op jit(solution)/shard_map/sublayer/pallas_call | solution.py:431
  43.0 0.7 %copy.11 = bf16[1,2,6,24,512]{4,3,2,1,0:T(8,128)(2,1)} copy(bf16[1,2,6,24,512]{4,3,2,1,0:T(8,128)(2,1)S(1)} %bitcast.5) | data formatting | bytes 589824
  43.7 0.6 %copy.12 = f32[4,512]{1,0:T(4,128)} copy(f32[4,512]{1,0:T(4,128)S(1)} %get-tuple-element.7) | data formatting | bytes 16384
